TPU v7x, 256 devices: a whole 4x4x8 slice. The times are simulated.
256 devices in a mesh: fsdp: 4 (over y_lo, core), ctx: 64 (over x, z, y_hi).
Axes of the slice: x: 4, y: 4 (y_hi: 2, y_lo: 2; y = y_hi * 2 + y_lo), z: 8, core: 2. Of those that a mesh axis runs over, the one named last changes fastest.
Arguments:
- hidden: bfloat16 [4, 8192, 2048], P('fsdp', 'ctx'), may hold values from -6 to 6
- queries: bfloat16 [4, 8192, 1024], P('fsdp', 'ctx'), may hold values from -6 to 6
- attn_out: bfloat16 [4, 8192, 1024], P('fsdp', 'ctx'), may hold values from -6 to 6
- grad_out: bfloat16 [4, 8192, 1024], P('fsdp', 'ctx'), may hold values from -6 to 6
- log_sums: float32 [4, 16, 8192], P('fsdp', None, 'ctx'), may hold values from 6 to 9
- block_order: int32 [4, 64], P('fsdp'), may hold values from 0 to 63, each once within a row
- w_kv: bfloat16 [2048, 512], P('fsdp'), may hold values from -0.125 to 0.125
Outputs:
- query_grads: bfloat16 [4, 8192, 1024], P('fsdp', 'ctx')
- input_grads: bfloat16 [4, 8192, 2048], P('fsdp', 'ctx')
- weight_grads: float32 [2048, 512], P(('fsdp', 'ctx'))
Inputs may be any that keep to these rules, and one draw needn't show every extreme that they name: Each row of block_order is a permutation of the 64 block numbers.
All inputs are finite; a program needn't handle non-finite values.
Results may differ from a plain program's by a relative error of at most 0.013.
The roundings to bfloat16 on the way count: a program that leaves them out, or rounds other values in their place, can miss the bound.
Values may be sent and summed in bfloat16 or wider, within the bound.
A program may use at most 128 MiB of HBM per device.

v0:
```python
import jax
import jax.numpy as jnp
from jax import lax
from jax.sharding import PartitionSpec as P

Q_HEADS = 16
KV_HEADS = 4
HEAD_DIM = 64


def shifted(array, axis, by):
    size = lax.axis_size(axis)
    return lax.ppermute(array, axis, [(i, (i + by) % size) for i in range(size)])


def shards(hidden, queries, attn_out, grad_out, log_sums, block_order, w_kv):
    rows_dev = hidden.shape[1]
    cycle_size = lax.axis_size("ctx")
    position = lax.axis_index("ctx")
    order_row = block_order[0]
    my_block = order_row[position]
    groups = Q_HEADS // KV_HEADS
    score_scale = HEAD_DIM ** (-0.5)
    key_width = KV_HEADS * HEAD_DIM
    w_all = lax.all_gather(w_kv, "fsdp", axis=0, tiled=True)
    inputs = hidden[0]
    key_vals = jnp.dot(inputs, w_all, preferred_element_type=jnp.float32).astype(jnp.bfloat16)
    query4 = queries[0].reshape(rows_dev, KV_HEADS, groups, HEAD_DIM)
    grad4 = grad_out[0].reshape(rows_dev, KV_HEADS, groups, HEAD_DIM)
    output4 = attn_out[0].reshape(rows_dev, KV_HEADS, groups, HEAD_DIM)
    delta4 = jnp.sum(grad4.astype(jnp.float32) * output4.astype(jnp.float32), axis=3).transpose(
        1, 2, 0
    )
    lse4 = log_sums[0].reshape(KV_HEADS, groups, rows_dev)

    def block_grads(key_block, causal_mask):
        key4 = key_block[:, :key_width].reshape(rows_dev, KV_HEADS, HEAD_DIM)
        value4 = key_block[:, key_width:].reshape(rows_dev, KV_HEADS, HEAD_DIM)
        scores = (
            jnp.einsum("qgnd,kgd->gnqk", query4, key4, preferred_element_type=jnp.float32)
            * score_scale
        )
        probs = jnp.exp(scores - lse4[..., None])
        if causal_mask is not None:
            probs = jnp.where(causal_mask, probs, 0.0)
        probs_low = probs.astype(jnp.bfloat16)
        value_grad = jnp.einsum(
            "gnqk,qgnd->kgd", probs_low, grad4, preferred_element_type=jnp.float32
        )
        prob_grad = jnp.einsum("qgnd,kgd->gnqk", grad4, value4, preferred_element_type=jnp.float32)
        score_grad = (probs * (prob_grad - delta4[..., None])).astype(jnp.bfloat16)
        query_grad = (
            jnp.einsum("gnqk,kgd->qgnd", score_grad, key4, preferred_element_type=jnp.float32)
            * score_scale
        )
        key_grad = (
            jnp.einsum("gnqk,qgnd->kgd", score_grad, query4, preferred_element_type=jnp.float32)
            * score_scale
        )
        return (
            query_grad.reshape(rows_dev, Q_HEADS * HEAD_DIM),
            jnp.concatenate(
                [key_grad.reshape(rows_dev, key_width), value_grad.reshape(rows_dev, key_width)],
                axis=1,
            ),
        )

    empty_query = jnp.zeros((rows_dev, Q_HEADS * HEAD_DIM), jnp.float32)
    empty_keys = jnp.zeros((rows_dev, 2 * key_width), jnp.float32)

    def visit(key_block, key_order):
        return lax.cond(
            key_order < my_block,
            lambda block_in: block_grads(block_in, None),
            lambda block_in: (empty_query, empty_keys),
            key_block,
        )

    row_ids = jnp.arange(rows_dev, dtype=jnp.int32)
    own_mask = row_ids[None, :] <= row_ids[:, None]
    own_query, own_keys = block_grads(key_vals, own_mask)
    ahead = cycle_size - 1

    def ahead_step(hop_index, state):
        key_buffer, grad_buffer, query_total = state
        key_buffer = shifted(key_buffer, "ctx", 1)
        grad_buffer = shifted(grad_buffer, "ctx", 1)
        query_part, keys_part = visit(key_buffer, order_row[(position - hop_index) % cycle_size])
        return (key_buffer, grad_buffer + keys_part, query_total + query_part)

    key_buffer, grad_buffer, query_total = lax.fori_loop(
        1, ahead + 1, ahead_step, (key_vals, own_keys, own_query)
    )
    key_grads = shifted(grad_buffer.astype(jnp.bfloat16), "ctx", -ahead).astype(grad_buffer.dtype)
    kv_grad = key_grads.astype(jnp.bfloat16)
    input_grads = jnp.dot(kv_grad, w_all.T, preferred_element_type=jnp.float32).astype(jnp.bfloat16)
    weight_grads = lax.psum_scatter(
        lax.dot_general(
            inputs, kv_grad, (((0,), (0,)), ((), ())), preferred_element_type=jnp.float32
        ),
        ("fsdp", "ctx"),
        scatter_dimension=0,
        tiled=True,
    )
    return (query_total.astype(jnp.bfloat16)[None], input_grads[None], weight_grads)


def solution(mesh):
    return jax.shard_map(
        shards,
        mesh=mesh,
        in_specs=(
            P("fsdp", "ctx", None),
            P("fsdp", "ctx", None),
            P("fsdp", "ctx", None),
            P("fsdp", "ctx", None),
            P("fsdp", None, "ctx"),
            P("fsdp", None),
            P("fsdp", None),
        ),
        out_specs=(P("fsdp", "ctx", None), P("fsdp", "ctx", None), P(("fsdp", "ctx"), None)),
        check_vma=False,
    )
```

profile of v0, /device:TPU:1, one launch (start us, length us, event | category | flops | bytes accessed | tf_op | source)
XLA Modules:
  0.0 2445.3 jit_solution(9408558689680880578)
XLA Ops:
  12.0 33.7 %all-gather.2.cloned.1.call-done = bf16[2048,512]{1,0:T(8,128)(2,1)} async-done(((bf16[512,512]{1,0:T(8,128)(2,1)}), bf16[2048,512]{1,0:T(8,128)(2,1)}) %all-gather.2.cloned.1.call-update) | async-done | bytes 2097168 | tf_op jit(solution)/shard_map/all_gather | solution.py:25
  49.8 957.6 %while.19 = (s32[]{:T(128)}, bf16[128,512]{0,1:T(8,128)(2,1)S(1)}, f32[128,512]{0,1:T(8,128)S(1)}, f32[128,1024]{0,1:T(8,128)S(1)}, s32[]{:T(128)}, /*index=5*/s...) while((s32[]{:T(128)}, bf16[128,512]{0,1:T(8,128)(2,1)S(1)}, ...), condition=%wide.region_4.5_spmd, body=%wide.region_1.4_spmd.sunk | while | flops 169771024 | bytes 11747786 | solution.py:91
  55.8 10.8 collective-permute-done
  70.7 13.4 collective-permute-done
  88.0 12.7 collective-permute-done
  104.6 13.3 collective-permute-done
  121.8 12.4 collective-permute-done
  136.6 10.3 collective-permute-done
  150.8 10.3 collective-permute-done
  165.0 10.3 collective-permute-done
  179.2 10.3 collective-permute-done
  193.4 10.3 collective-permute-done
  207.7 10.3 collective-permute-done
  221.9 10.3 collective-permute-done
  234.6 10.5 collective-permute-done
  249.0 11.6 collective-permute-done
  264.5 12.7 collective-permute-done
  281.1 13.7 collective-permute-done
  298.7 13.4 collective-permute-done
  316.0 14.7 collective-permute-done
  334.7 13.9 collective-permute-done
  352.5 14.6 collective-permute-done
  369.5 12.1 collective-permute-done
  385.5 12.7 collective-permute-done
  402.2 11.8 collective-permute-done
  417.9 12.4 collective-permute-done
  432.7 10.3 collective-permute-done
  530.6 10.5 collective-permute-done
  601.9 10.3 collective-permute-done
  628.8 10.9 collective-permute-done
  642.1 12.0 collective-permute-done
  658.0 13.1 collective-permute-done
  675.0 14.2 collective-permute-done
  691.6 14.0 collective-permute-done
  709.5 14.6 collective-permute-done
  726.5 13.8 collective-permute-done
  744.2 12.8 collective-permute-done
  761.0 11.9 collective-permute-done
  776.8 11.0 collective-permute-done
  803.0 10.3 collective-permute-done
  874.0 10.3 collective-permute-done
  915.1 10.3 collective-permute-done
  929.3 10.8 collective-permute-done
  944.0 11.8 collective-permute-done
  959.8 12.9 collective-permute-done
  975.1 13.8 collective-permute-done
  992.8 12.9 collective-permute-done
  1029.2 1409.3 %reduce-scatter.4.cloned.1.call-done = f32[8,512]{1,0:T(8,128)} async-done(((f32[2048,512]{1,0:T(8,128)}), f32[8,512]{1,0:T(8,128)}) %reduce-scatter.4.cloned.1.call-update) | async-done | bytes 16400
  (932 shorter events, 438.6 us)
Async XLA Ops:
  7.2 38.6 %all-gather.2.cloned.1.call-start = ((), (), s32[]{:S(2)}) async-start(), calls=%async_computation.1 | async-start | bytes 2621440 | tf_op jit(solution)/shard_map/all_gather | solution.py:25
  7.9 2430.6 %reduce-scatter.4.cloned.1.call-start = ((), (), s32[]{:S(2)}) async-start(), calls=%async_computation.2 | async-start | bytes 4210688
  49.8 18.5 collective-permute-start.1
  68.4 17.5 collective-permute-start.1
  68.4 15.7 collective-permute-start
  85.9 16.6 collective-permute-start.1
  86.0 14.7 collective-permute-start
  102.5 17.1 collective-permute-start.1
  102.6 15.3 collective-permute-start
  119.7 14.7 collective-permute-start.1
  246.8 15.4 collective-permute-start.1
  262.3 16.5 collective-permute-start.1
  278.9 17.6 collective-permute-start.1
  279.0 15.8 collective-permute-start
  296.6 17.3 collective-permute-start.1
  296.7 15.5 collective-permute-start
  313.9 18.6 collective-permute-start.1
  314.0 16.8 collective-permute-start
  332.6 17.8 collective-permute-start.1
  332.7 15.9 collective-permute-start
  350.4 16.9 collective-permute-start.1
  350.5 16.6 collective-permute-start
  367.3 16.0 collective-permute-start.1
  383.4 16.6 collective-permute-start.1
  383.5 14.8 collective-permute-start
  400.0 15.7 collective-permute-start.1
  415.8 14.7 collective-permute-start.1
  640.0 15.9 collective-permute-start.1
  655.9 16.9 collective-permute-start.1
  656.0 15.1 collective-permute-start
  672.9 16.5 collective-permute-start.1
  673.0 16.2 collective-permute-start
  689.5 17.8 collective-permute-start.1
  689.6 16.0 collective-permute-start
  707.4 17.0 collective-permute-start.1
  707.5 16.7 collective-permute-start
  724.4 17.6 collective-permute-start.1
  724.5 15.8 collective-permute-start
  742.1 16.7 collective-permute-start.1
  742.2 14.9 collective-permute-start
  758.9 15.8 collective-permute-start.1
  941.9 15.7 collective-permute-start.1
  957.6 15.3 collective-permute-start.1
  957.7 15.0 collective-permute-start
  973.0 17.6 collective-permute-start.1
  973.1 15.8 collective-permute-start
  990.7 16.7 collective-permute-start.1
  990.8 14.9 collective-permute-start
  (84 other events, 1150.9 us)
Sparse Core Ops, SparseCore 0:
  9.8 35.8 all-gather.1
  1025.3 1413.1 reduce-scatter.3
where the time goes:
time: 2450 us
  waiting for transfers between devices  2180 us (89%)
  loops' own time  87.9 us (4%)
  matrix products  85 us (3%)
  local copies, waits for them, and re-layouts  53.3 us (2%)
    unnamed x3, waiting for transfers between devices  1410 us
    ppermute x127, waiting for transfers between devices, shifted(): lax.ppermute(array, axis, [(i, (i + by) % size) for i in range(size)])  736 us
    another operation x1, loops' own time, shards(): lax.fori_loop(1, ahead + 1, ahead_step, (key_vals, own_keys, own_query))  86 us
  transfers between devices with their start and end apart: 129, of which 66 were waited for; matrix products, arithmetic and copies ran while one was open for 5% of the time, Pallas kernels for 0%

commit v1 on v0

v1 whole, which is shorter than its diff:
```python
import functools

import jax
import jax.numpy as jnp
from jax import lax
from jax.experimental import pallas as pl
from jax.experimental.pallas import tpu as pltpu
from jax.sharding import PartitionSpec as P

BF, F32 = jnp.bfloat16, jnp.float32
NT = (((1,), (1,)), ((), ()))
TN = (((0,), (0,)), ((), ()))
MESH = pl.DeviceIdType.MESH
Q_HEADS, KV_HEADS, HEAD_DIM = 16, 4, 64
NX, NZ = 4, 8
VMEM = pl.BlockSpec(memory_space=pltpu.VMEM)
SMEM = pl.BlockSpec(memory_space=pltpu.SMEM)


def place():
    f, c = lax.axis_index("fsdp"), lax.axis_index("ctx")
    return c // 16, (c // 2) % 8, c % 2, f // 2, f % 2


def dev(x, z, hi, lo, core):
    return {"fsdp": lo * 2 + core, "ctx": (x * 8 + z) * 2 + hi}


def rcopy(src, dst, send, recv, to):
    return pltpu.make_async_remote_copy(
        src_ref=src, dst_ref=dst, send_sem=send, recv_sem=recv, device_id=to, device_id_type=MESH
    )


def greet(to):
    pl.semaphore_signal(pltpu.get_barrier_semaphore(), inc=1, device_id=to, device_id_type=MESH)


def spread_kernel(
    hid, w, q, do, stat,
    q_buf, do_buf, stat_buf, kv_buf, w_all, hid_buf,
    kvs, acc, qs_sem, ks_sem, ws_sem, hs_sem, fs_sem, qr_sem, kr_sem, wr_sem, hr_sem, fr_sem, zs_sem, zr_sem,
):
    x, z, hi, lo, core = place()
    f = lo * 2 + core
    me = dev(x, z, hi, lo, core)
    sib = dev(x, z, hi, lo, 1 - core)
    near = dev(x, z, hi, 1 - lo, core)
    across = dev(x, z, hi, 1 - lo, 1 - core)
    far = dev(x, z, 1 - hi, 1 - lo, core)
    up, down = dev(x, (z + 1) % NZ, hi, lo, core), dev(x, (z + 7) % NZ, hi, lo, core)
    own = hi == core

    for to in (sib, near, across, far, up, down):
        greet(to)

    def greet_q(i, c):
        greet(dev((x + i // NZ) % NX, (z + i) % NZ, 1 - core, lo, hi))
        return c

    lax.fori_loop(0, 32, greet_q, 0)

    def greet_kv(i, c):
        dx, h = i // 2, i % 2

        @pl.when(jnp.logical_not((dx == 0) & own & (h == hi)))
        def _():
            greet(dev((x + dx) % NX, z, h, lo, hi))

        return c

    lax.fori_loop(0, 8, greet_kv, 0)
    pl.semaphore_wait(pltpu.get_barrier_semaphore(), 6 + 32 + 8 - own.astype(jnp.int32))

    w_own = pltpu.make_async_copy(w, w_all.at[f], ws_sem.at[3])
    w_own.start()
    half = w.shape[0] // 2
    w_sends = [
        rcopy(w.at[pl.ds(0, half)], w_all.at[f, pl.ds(0, half)], ws_sem.at[0], wr_sem.at[0], near),
        rcopy(w.at[pl.ds(half, half)], w_all.at[f, pl.ds(half, half)], ws_sem.at[1], wr_sem.at[1], far),
        rcopy(w, w_all.at[f], ws_sem.at[2], wr_sem.at[2], sib),
    ]
    for c in w_sends:
        c.start()

    slot = hi * 32 + x * 8 + z

    def q_copies(i):
        tx, tz = (x + i // NZ) % NX, (z + i) % NZ
        to = dev(tx, tz, core, lo, 1 - hi)
        rows, cols = pl.ds(pl.multiple_of(tz * 16, 16), 16), pl.ds(pl.multiple_of(tx * 256, 256), 256)
        return (
            rcopy(q.at[rows, cols], q_buf.at[slot], qs_sem.at[0], qr_sem.at[0], to),
            rcopy(do.at[rows, cols], do_buf.at[slot], qs_sem.at[1], qr_sem.at[1], to),
            rcopy(stat.at[tx, tz], stat_buf.at[slot], qs_sem.at[2], qr_sem.at[2], to),
        )

    def send_q(i, c):
        for copy in q_copies(i):
            copy.start()
        return c

    lax.fori_loop(0, 32, send_q, 0)

    def project(chunk):
        cols = pl.ds(pl.multiple_of(chunk * 512, 512), 512)
        return jnp.dot(hid[:, cols], w_all[chunk], preferred_element_type=F32)

    w_own.wait()
    acc[...] = project(f)
    w_sends[2].wait_recv()
    acc[...] += project(lo * 2 + 1 - core)
    other = (1 - lo) * 2 + core
    fwd = []
    for i in range(2):
        part = pl.ds(i * half, half)
        rcopy(w_all.at[other, part], w_all.at[other, part], ws_sem.at[i], wr_sem.at[i], near).wait_recv()
        c = rcopy(w_all.at[other, part], w_all.at[other, part], fs_sem.at[i], fr_sem.at[i], sib)
        c.start()
        fwd.append(c)
    acc[...] += project(other)
    last = (1 - lo) * 2 + 1 - core
    for i in range(2):
        part = pl.ds(i * half, half)
        rcopy(w_all.at[last, part], w_all.at[last, part], fs_sem.at[i], fr_sem.at[i], sib).wait_recv()
    key_vals = (acc[...] + project(last)).astype(BF)
    for g in range(KV_HEADS):
        kvs[g] = jnp.concatenate(
            [key_vals[:, g * 64 : g * 64 + 64], key_vals[:, 256 + g * 64 : 320 + g * 64]], axis=1
        )

    kslot = z * 8 + x * 2 + hi

    def kv_copy(dx, j):
        tx = (x + dx) % NX
        return rcopy(
            kvs.at[tx, pl.ds(j * 64, 64)], kv_buf.at[kslot], ks_sem.at[0], kr_sem.at[0], dev(tx, z, core, lo, j)
        )

    def kv_local(j):
        return pltpu.make_async_copy(kvs.at[x, pl.ds(j * 64, 64)], kv_buf.at[kslot], ks_sem.at[1])

    for dx in range(NX):
        for j in range(2):
            if dx > 0:
                kv_copy(dx, j).start()
            else:
                mine = own & (core == j)

                @pl.when(jnp.logical_not(mine))
                def _():
                    kv_copy(dx, j).start()

                @pl.when(mine)
                def _():
                    kv_local(j).start()

    def hid_copy(i, to, tf):
        cols = pl.ds(pl.multiple_of(tf * 512, 512), 512)
        return rcopy(hid.at[:, cols], hid_buf.at[f], hs_sem.at[i], hr_sem.at[i], to)

    hid_sends = [
        hid_copy(0, sib, lo * 2 + 1 - core),
        hid_copy(1, near, other),
        hid_copy(2, across, last),
    ]
    for c in hid_sends:
        c.start()
    hid_own = pltpu.make_async_copy(
        hid.at[:, pl.ds(pl.multiple_of(f * 512, 512), 512)], hid_buf.at[f], hs_sem.at[3]
    )
    hid_own.start()

    @pl.when(own)
    def _():
        pltpu.make_async_copy(kv_buf.at[0], kv_buf.at[0], ks_sem.at[1]).wait()
        rcopy(kv_buf.at[pl.ds(0, 7)], kv_buf.at[pl.ds(0, 7)], ks_sem.at[0], kr_sem.at[0], up).wait_recv()

    @pl.when(jnp.logical_not(own))
    def _():
        rcopy(kv_buf.at[pl.ds(0, 8)], kv_buf.at[pl.ds(0, 8)], ks_sem.at[0], kr_sem.at[0], up).wait_recv()

    def z_copy(d, s, src_z, to):
        part = kv_buf.at[pl.ds(pl.multiple_of(src_z * 8, 8), 8)]
        return rcopy(part, part, zs_sem.at[d, s], zr_sem.at[d, s], to)

    z_sends = []
    for s in range(4):
        if s:
            z_copy(0, s - 1, (z + 8 - s) % NZ, up).wait_recv()
        c = z_copy(0, s, (z + 8 - s) % NZ, up)
        c.start()
        z_sends.append(c)
        if s < 3:
            if s:
                z_copy(1, s - 1, (z + s) % NZ, down).wait_recv()
            c = z_copy(1, s, (z + s) % NZ, down)
            c.start()
            z_sends.append(c)

    got = pl.ds(pl.multiple_of((1 - core) * 32, 32), 32)
    theirs = pl.ds(pl.multiple_of(core * 32, 32), 32)
    bufs = (q_buf, do_buf, stat_buf)
    for i, buf in enumerate(bufs):
        rcopy(buf.at[got], buf.at[got], qs_sem.at[i], qr_sem.at[i], sib).wait_recv()
        c = rcopy(buf.at[got], buf.at[got], fs_sem.at[2 + i], fr_sem.at[2 + i], sib)
        c.start()
        fwd.append(c)
    for i, buf in enumerate(bufs):
        rcopy(buf.at[theirs], buf.at[theirs], fs_sem.at[2 + i], fr_sem.at[2 + i], sib).wait_recv()

    z_copy(0, 3, (z + 4) % NZ, up).wait_recv()
    z_copy(1, 2, (z + 3) % NZ, down).wait_recv()
    hid_own.wait()
    for i, src in enumerate((lo * 2 + 1 - core, other, last)):
        rcopy(hid_buf.at[src], hid_buf.at[src], hs_sem.at[i], hr_sem.at[i], sib).wait_recv()
    for c in hid_sends + z_sends + fwd + w_sends:
        c.wait_send()

    def done_q(i, c):
        for copy in q_copies(i):
            copy.wait_send()
        return c

    lax.fori_loop(0, 32, done_q, 0)

    for dx in range(NX):
        for j in range(2):
            if dx > 0:
                kv_copy(dx, j).wait_send()
            else:

                @pl.when(jnp.logical_not(own & (core == j)))
                def _():
                    kv_copy(dx, j).wait_send()


def spread(hid, w, q, do, stat):
    dma = pltpu.SemaphoreType.DMA
    return pl.pallas_call(
        spread_kernel,
        name="spread",
        out_shape=(
            jax.ShapeDtypeStruct((64, 16, 256), BF),
            jax.ShapeDtypeStruct((64, 16, 256), BF),
            jax.ShapeDtypeStruct((64, 1, 128), F32),
            jax.ShapeDtypeStruct((64, 64, 128), BF),
            jax.ShapeDtypeStruct((4, 512, 512), BF),
            jax.ShapeDtypeStruct((4, 128, 512), BF),
        ),
        in_specs=[VMEM] * 5,
        out_specs=[VMEM] * 6,
        scratch_shapes=[
            pltpu.VMEM((4, 128, 128), BF),
            pltpu.VMEM((128, 512), F32),
            dma((3,)), dma((2,)), dma((4,)), dma((4,)), dma((5,)),
            dma((3,)), dma((1,)), dma((3,)), dma((3,)), dma((5,)),
            dma((2, 4)), dma((2, 4)),
        ],
        compiler_params=pltpu.CompilerParams(
            collective_id=0, has_side_effects=True, vmem_limit_bytes=40 * 2**20
        ),
    )(hid, w, q, do, stat)


def attn_kernel(
    geo, order, q_ref, do_ref, stat_ref, kv_ref, dq_ref, dkv_ref,
    inv, qz, dz, kvs, kts, lse, dlt, dqt, dkv,
):
    zoff, koff = geo[0] * 16, geo[1] * 64

    def put(i, c):
        for j in range(8):
            inv[order[i * 8 + j]] = i * 8 + j
        return c

    lax.fori_loop(0, 8, put, 0)
    low = lax.broadcasted_iota(jnp.int32, (16, 128), 1) < 64
    low1 = lax.broadcasted_iota(jnp.int32, (1, 128), 1) < 64

    def q_slot(b):
        return lax.rem(b, 2) * 32 + lax.div(b, 2)

    def k_slot(b):
        c = lax.div(b, 2)
        return lax.rem(c, 8) * 8 + lax.div(c, 8) * 2 + lax.rem(b, 2)

    def sort(blk, c):
        stats = []
        for off in range(8):
            b = inv[blk * 8 + off]
            s = q_slot(b)
            for hp in range(2):
                qq = q_ref[s, :, hp * 128 : (hp + 1) * 128].astype(F32) * 0.125
                dd = do_ref[s, :, hp * 128 : (hp + 1) * 128].astype(F32)
                for ho in range(2):
                    rows = slice(off * 64 + hp * 32 + ho * 16, off * 64 + hp * 32 + ho * 16 + 16)
                    qh = qq if ho == 0 else pltpu.roll(qq, 64, 1)
                    dh = dd if ho == 1 else pltpu.roll(dd, 64, 1)
                    qz[blk, rows, :] = jnp.where(low, qh, 0.0).astype(BF)
                    dz[blk, rows, :] = jnp.where(low, 0.0, dh).astype(BF)
            kvs[blk, off * 64 : off * 64 + 64, :] = kv_ref[k_slot(b)]
            stats.append(stat_ref[s])
        for j in range(4):
            a, b = stats[2 * j], stats[2 * j + 1]
            lse[blk, :, j * 128 : (j + 1) * 128] = jnp.where(low1, a, pltpu.roll(b, 64, 1))
            dlt[blk, :, j * 128 : (j + 1) * 128] = jnp.where(low1, pltpu.roll(a, 64, 1), b)
        kts[blk] = kvs[blk].astype(F32).T[:64].astype(BF)
        dqt[blk] = jnp.zeros((64, 512), F32)
        dkv[blk] = jnp.zeros((512, 128), F32)
        return c

    lax.fori_loop(0, 8, sort, 0)

    def tile(m, c, diag):
        q, d, l, dl = qz[c], dz[c], lse[c], dlt[c]
        for a in range(2):
            keys = slice(a * 256, (a + 1) * 256)
            kv = kvs[m, keys, :]
            p = jnp.exp(lax.dot_general(kv, q, NT, preferred_element_type=F32) - l)
            if diag:
                kp = lax.broadcasted_iota(jnp.int32, (256, 512), 0) + a * 256
                qp = lax.broadcasted_iota(jnp.int32, (256, 512), 1)
                kpos = (kp // 64) * 128 + (kp % 64) + koff
                qpos = (qp // 64) * 128 + (qp % 16) + zoff
                p = jnp.where(kpos <= qpos, p, 0.0)
            dp = lax.dot_general(kv, d, NT, preferred_element_type=F32)
            ds = (p * (dp - dl)).astype(BF)
            dkv[m, keys, :] += jnp.dot(ds, q, preferred_element_type=F32) + jnp.dot(
                p.astype(BF), d, preferred_element_type=F32
            )
            dqt[c] += jnp.dot(kts[m, :, keys], ds, preferred_element_type=F32)

    def outer(m, carry):
        tile(m, m, True)

        def inner(c, carry):
            tile(m, c, False)
            return carry

        return lax.fori_loop(m + 1, 8, inner, carry)

    lax.fori_loop(0, 8, outer, 0)

    def finish(blk, c):
        for j in range(4):
            t = (dqt[blk, :, j * 128 : (j + 1) * 128] * 0.125).T
            for o in range(2):
                b = inv[blk * 8 + j * 2 + o]
                dq_ref[q_slot(b)] = jnp.concatenate(
                    [t[o * 64 + h * 16 : o * 64 + h * 16 + 16] for h in range(4)], axis=1
                )
                off = j * 2 + o
                dkv_ref[k_slot(b)] = dkv[blk, off * 64 : off * 64 + 64, :]
        return c

    lax.fori_loop(0, 8, finish, 0)


def attn(geo, order, q, do, stat, kv):
    return pl.pallas_call(
        attn_kernel,
        name="attn",
        out_shape=(jax.ShapeDtypeStruct((64, 16, 256), F32), jax.ShapeDtypeStruct((64, 64, 128), F32)),
        in_specs=[SMEM, SMEM, VMEM, VMEM, VMEM, VMEM],
        out_specs=(VMEM, VMEM),
        scratch_shapes=[
            pltpu.SMEM((64,), jnp.int32),
            pltpu.VMEM((8, 512, 128), BF),
            pltpu.VMEM((8, 512, 128), BF),
            pltpu.VMEM((8, 512, 128), BF),
            pltpu.VMEM((8, 64, 512), BF),
            pltpu.VMEM((8, 1, 512), F32),
            pltpu.VMEM((8, 1, 512), F32),
            pltpu.VMEM((8, 64, 512), F32),
            pltpu.VMEM((8, 512, 128), F32),
        ],
        compiler_params=pltpu.CompilerParams(vmem_limit_bytes=50 * 2**20),
    )(geo, order, q, do, stat, kv)


def collect_kernel(
    dq, dkv, w_all, hid_buf, dq_out, in_out, wg_out,
    dq_rx, dq_tx, rs_tx, rs_rx, fin, kvg, kvn, wpart, wx_rx, wz, wz_rx, wy, wy_rx,
    as_sem, ar_sem, qs_sem, qr_sem, zs_sem, zr_sem, ks_sem, kr_sem, fs_sem, fr_sem,
    xs_sem, xr_sem, vs_sem, vr_sem, ys_sem, yr_sem,
):
    x, z, hi, lo, core = place()
    f = lo * 2 + core
    sib = dev(x, z, hi, lo, 1 - core)
    near = dev(x, z, hi, 1 - lo, core)
    across = dev(x, z, hi, 1 - lo, 1 - core)
    pair = dev(x, z, 1 - hi, lo, core)
    up, down = dev(x, (z + 1) % NZ, hi, lo, core), dev(x, (z + 7) % NZ, hi, lo, core)
    own = hi == core

    def xdev(i):
        return dev((x + i) % NX, z, hi, lo, core)

    def zdev(i):
        return dev(x, (z + i) % NZ, hi, lo, core)

    for to in (sib, near, across, pair):
        greet(to)
    for i in range(1, NX):
        greet(xdev(i))
    for i in range(1, NZ):
        greet(zdev(i))

    def greet_q(i, c):
        greet(dev((x + i // NZ) % NX, (z + i) % NZ, core, lo, 1 - hi))
        return c

    lax.fori_loop(0, 32, greet_q, 0)

    def greet_kv(i, c):
        dx, j = i // 2, i % 2

        @pl.when(jnp.logical_not((dx == 0) & own & (j == core)))
        def _():
            greet(dev((x + dx) % NX, z, core, lo, j))

        return c

    lax.fori_loop(0, 8, greet_kv, 0)
    pl.semaphore_wait(pltpu.get_barrier_semaphore(), 4 + 3 + 7 + 32 + 8 - own.astype(jnp.int32))

    theirs = pl.ds(pl.multiple_of(core * 32, 32), 32)
    a = rcopy(dq.at[theirs], dq_rx, as_sem, ar_sem, sib)
    a.start()

    def z_send(d, s, src_z, to):
        terms = dkv[pl.ds(pl.multiple_of(src_z * 8, 8), 8)]
        if s:
            rcopy(rs_tx.at[d, s], rs_rx.at[d, s - 1], zs_sem.at[d, s - 1], zr_sem.at[d, s - 1], to).wait_recv()
            terms = terms + rs_rx[d, s - 1].astype(F32)
        rs_tx[d, s] = terms.astype(BF)
        c = rcopy(rs_tx.at[d, s], rs_rx.at[d, s], zs_sem.at[d, s], zr_sem.at[d, s], to)
        c.start()
        return c

    sends = []
    q_started = False
    for s in range(4):
        sends.append(z_send(0, s, (z + 4 - s) % NZ, up))
        if s < 3:
            sends.append(z_send(1, s, (z + 5 + s) % NZ, down))
        if s == 0:
            a.wait_recv()

            def add_q(i, c):
                for j in range(4):
                    k = i * 4 + j
                    dq_tx[k] = (dq[(1 - core) * 32 + k] + dq_rx[k]).astype(BF)
                return c

            lax.fori_loop(0, 8, add_q, 0)
            rows, cols = pl.ds(pl.multiple_of(z * 16, 16), 16), pl.ds(pl.multiple_of(x * 256, 256), 256)

            def q_copy(i):
                tx, tz = (x + i // NZ) % NX, (z + i) % NZ
                return rcopy(
                    dq_tx.at[tx * 8 + tz], dq_out.at[rows, cols], qs_sem, qr_sem, dev(tx, tz, 1 - core, lo, hi)
                )

            def send_q(i, c):
                q_copy(i).start()
                return c

            lax.fori_loop(0, 32, send_q, 0)

    rcopy(rs_tx.at[0, 3], rs_rx.at[0, 3], zs_sem.at[0, 3], zr_sem.at[0, 3], up).wait_recv()
    rcopy(rs_tx.at[1, 2], rs_rx.at[1, 2], zs_sem.at[1, 2], zr_sem.at[1, 2], down).wait_recv()
    fin[...] = (
        dkv[pl.ds(pl.multiple_of(z * 8, 8), 8)] + rs_rx[0, 3].astype(F32) + rs_rx[1, 2].astype(F32)
    ).astype(BF)

    krows = pl.ds(pl.multiple_of(core * 64, 64), 64)

    def kv_copy(dx, h):
        tx = (x + dx) % NX
        return rcopy(
            fin.at[tx * 2 + h], kvg.at[f_of(), x, krows], ks_sem.at[0], kr_sem.at[0], dev(tx, z, h, lo, hi)
        )

    def f_of():
        return lo * 2 + hi

    def kv_local(h):
        return pltpu.make_async_copy(fin.at[x * 2 + h], kvg.at[f_of(), x, krows], ks_sem.at[1])

    for dx in range(NX):
        for h in range(2):
            if dx > 0:
                kv_copy(dx, h).start()
            else:
                mine = own & (hi == h)

                @pl.when(jnp.logical_not(mine))
                def _():
                    kv_copy(dx, h).start()

                @pl.when(mine)
                def _():
                    kv_local(h).start()

    blk8 = kvg.at[0, :, pl.ds(0, 128)]

    @pl.when(own)
    def _():
        kv_local(0).wait()
        part = fin.at[pl.ds(0, 7)]
        rcopy(part, part, ks_sem.at[0], kr_sem.at[0], up).wait_recv()

    @pl.when(jnp.logical_not(own))
    def _():
        rcopy(fin, fin, ks_sem.at[0], kr_sem.at[0], up).wait_recv()

    for i, to in enumerate((sib, near, across)):
        c = rcopy(kvg.at[f], kvg.at[f], fs_sem.at[i], fr_sem.at[i], to)
        c.start()
        sends.append(c)

    def natural(i):
        kvn[i] = jnp.concatenate(
            [kvg[i, g, :, :64] for g in range(4)] + [kvg[i, g, :, 64:] for g in range(4)], axis=1
        )

    natural(f)
    for i in range(4):
        in_out[:, i * 512 : (i + 1) * 512] = lax.dot_general(
            kvn[f], w_all[i], NT, preferred_element_type=F32
        ).astype(BF)

    def grad_w(i):
        return lax.dot_general(hid_buf[i], kvn[i], TN, preferred_element_type=F32)

    wpart[...] = grad_w(f)
    for i, src in enumerate((lo * 2 + 1 - core, (1 - lo) * 2 + core, (1 - lo) * 2 + 1 - core)):
        rcopy(kvg.at[src], kvg.at[src], fs_sem.at[i], fr_sem.at[i], sib).wait_recv()
        natural(src)
        wpart[...] += grad_w(src)

    for i in range(1, NX):
        tx = (x + i) % NX
        c = rcopy(
            wpart.at[pl.ds(pl.multiple_of(tx * 128, 128), 128)], wx_rx.at[i - 1],
            xs_sem.at[i - 1], xr_sem.at[i - 1], xdev(i),
        )
        c.start()
        sends.append(c)
    total = wpart[pl.ds(pl.multiple_of(x * 128, 128), 128), :]
    for i in range(1, NX):
        rcopy(wx_rx.at[i - 1], wx_rx.at[i - 1], xs_sem.at[i - 1], xr_sem.at[i - 1], sib).wait_recv()
        total = total + wx_rx[i - 1]
    wz[...] = total
    for i in range(1, NZ):
        tz = (z + i) % NZ
        c = rcopy(
            wz.at[pl.ds(pl.multiple_of(tz * 16, 16), 16)], wz_rx.at[i - 1],
            vs_sem.at[i - 1], vr_sem.at[i - 1], zdev(i),
        )
        c.start()
        sends.append(c)
    total = wz[pl.ds(pl.multiple_of(z * 16, 16), 16), :]
    for i in range(1, NZ):
        rcopy(wz_rx.at[i - 1], wz_rx.at[i - 1], vs_sem.at[i - 1], vr_sem.at[i - 1], sib).wait_recv()
        total = total + wz_rx[i - 1]
    wy[...] = total
    c = rcopy(wy.at[pl.ds(pl.multiple_of((1 - hi) * 8, 8), 8)], wy_rx, ys_sem, yr_sem, pair)
    c.start()
    sends.append(c)
    c.wait_recv()
    wg_out[...] = wy[pl.ds(pl.multiple_of(hi * 8, 8), 8), :] + wy_rx[...]

    rcopy(dq_tx, dq_tx, qs_sem, qr_sem, sib).wait_recv()
    for c in sends + [a]:
        c.wait_send()

    def done_q(i, c):
        q_copy(i).wait_send()
        return c

    lax.fori_loop(0, 32, done_q, 0)
    for dx in range(NX):
        for h in range(2):
            if dx > 0:
                kv_copy(dx, h).wait_send()
            else:

                @pl.when(jnp.logical_not(own & (hi == h)))
                def _():
                    kv_copy(dx, h).wait_send()


def collect(dq, dkv, w_all, hid_buf):
    dma = pltpu.SemaphoreType.DMA
    return pl.pallas_call(
        collect_kernel,
        name="collect",
        out_shape=(
            jax.ShapeDtypeStruct((128, 1024), BF),
            jax.ShapeDtypeStruct((128, 2048), BF),
            jax.ShapeDtypeStruct((8, 512), F32),
        ),
        in_specs=[VMEM] * 4,
        out_specs=[VMEM] * 3,
        scratch_shapes=[
            pltpu.VMEM((32, 16, 256), F32),
            pltpu.VMEM((32, 16, 256), BF),
            pltpu.VMEM((2, 4, 8, 64, 128), BF),
            pltpu.VMEM((2, 4, 8, 64, 128), BF),
            pltpu.VMEM((8, 64, 128), BF),
            pltpu.VMEM((4, 4, 128, 128), BF),
            pltpu.VMEM((4, 128, 512), BF),
            pltpu.VMEM((512, 512), F32),
            pltpu.VMEM((3, 128, 512), F32),
            pltpu.VMEM((128, 512), F32),
            pltpu.VMEM((7, 16, 512), F32),
            pltpu.VMEM((16, 512), F32),
            pltpu.VMEM((8, 512), F32),
            dma, dma, dma, dma, dma((2, 4)), dma((2, 4)), dma((2,)), dma((1,)), dma((3,)), dma((3,)),
            dma((3,)), dma((3,)), dma((7,)), dma((7,)), dma, dma,
        ],
        compiler_params=pltpu.CompilerParams(
            collective_id=1, has_side_effects=True, vmem_limit_bytes=50 * 2**20
        ),
    )(dq, dkv, w_all, hid_buf)


def shards(hidden, queries, attn_out, grad_out, log_sums, block_order, w_kv):
    x, z, hi, lo, core = place()
    delta = jnp.sum(
        (grad_out[0].astype(F32) * attn_out[0].astype(F32)).reshape(128, Q_HEADS, HEAD_DIM), axis=2
    ).T

    def sliced(a):
        return a.reshape(4, 4, 8, 16).transpose(0, 2, 1, 3).reshape(4, 8, 64)

    stat = jnp.concatenate([sliced(log_sums[0]), sliced(delta)], axis=2).reshape(4, 8, 1, 128)
    orders = lax.all_gather(block_order[0], "fsdp", axis=0)
    order = orders[lo * 2 + hi]
    geo = jnp.stack([z, core]).astype(jnp.int32)
    q, do, st, kv, w_all, hid_buf = spread(hidden[0], w_kv, queries[0], grad_out[0], stat)
    dq, dkv = attn(geo, order, q, do, st, kv)
    dq_out, in_out, wg = collect(dq, dkv, w_all, hid_buf)
    return dq_out[None], in_out[None], wg


def solution(mesh):
    return jax.shard_map(
        shards,
        mesh=mesh,
        in_specs=(
            P("fsdp", "ctx", None),
            P("fsdp", "ctx", None),
            P("fsdp", "ctx", None),
            P("fsdp", "ctx", None),
            P("fsdp", None, "ctx"),
            P("fsdp", None),
            P("fsdp", None),
        ),
        out_specs=(P("fsdp", "ctx", None), P("fsdp", "ctx", None), P(("fsdp", "ctx"), None)),
        check_vma=False,
    )
```

time: 2450 us -> 163 us (0.07)
  waiting for transfers between devices: 2180 us -> 0 us
  Pallas kernels: 0 us -> 145 us
  loops' own time: 87.9 us -> 0 us
  matrix products: 85 us -> 0 us
  local copies, waits for them, and re-layouts: 53.3 us -> 6.73 us
    unnamed x3 -> x0, waiting for transfers between devices: 1410 us -> none
    ppermute x127 -> x0, waiting for transfers between devices: 736 us -> none  [shifted(): lax.ppermute(array, axis, [(i, (i + by) % size) for i in range(size)])]
    pallas_call x0 -> x3, Pallas kernels: none -> 145 us  [the longest x1 68.9 us: collect(): pl.pallas_call(collect_kernel, name='collect', out_shape=(jax.ShapeDtypeS...]
    another operation x64 -> x0, loops' own time: 87.9 us -> none  [the longest x1 86 us: shards(): lax.fori_loop(1, ahead + 1, ahead_step, (key_vals, own_keys, own_query))]
    dot_general x258 -> x0, matrix products: 85 us -> none  [the longest x51 18 us: block_grads(): jnp.einsum('qgnd,kgd->gnqk', query4, key4, preferred_element_type=jnp.flo...]
    dynamic_slice x64 -> x0, local copies, waits for them, and re-layouts: 41.6 us -> none  [the longest x63 41 us: ahead_step(): order_row[(position - hop_index) % cycle_size]]
    all_gather x1 -> x0, waiting for transfers between devices: 33.7 us -> none  [shards(): w_all = lax.all_gather(w_kv, 'fsdp', axis=0, tiled=True)]
  transfers between devices with their start and end apart: 129 -> 0, of which waited for: 66 -> 0; matrix products, arithmetic and copies ran while one was open for 5% -> 0% of each run, Pallas kernels for 0% -> 0%
where the time goes in v1:
time: 163 us; the launch traced here: 161 us
  Pallas kernels  145 us (89%)
  blocking collectives  8.33 us (5%)
  local copies, waits for them, and re-layouts  6.73 us (4%)
    pallas_call x1, Pallas kernels, collect(): pl.pallas_call(collect_kernel, name='collect', out_shape=(jax.ShapeDtypeS...  68.9 us
    pallas_call x1, Pallas kernels, spread(): pl.pallas_call(spread_kernel, name='spread', out_shape=(jax.ShapeDtypeStr...  42.1 us
    pallas_call x1, Pallas kernels, attn(): pl.pallas_call(attn_kernel, name='attn', out_shape=(jax.ShapeDtypeStruct(...  34.3 us
    all_gather x1, blocking collectives, shards(): orders = lax.all_gather(block_order[0], 'fsdp', axis=0)  8.33 us
    unnamed x15, local copies, waits for them, and re-layouts  5.66 us

profile of v1, /device:TPU:1, one launch (start us, length us, event | category | flops | bytes accessed | tf_op | source)
XLA Modules:
  0.0 161.4 jit_solution(18286060929098498883)
XLA Ops:
  0.6 0.0 copy-start.1
  0.6 0.0 copy-start.3
  0.7 0.0 copy-start.4
  0.7 0.0 copy-start.2
  0.7 0.1 pad_add_fusion.geo
  0.8 8.3 %all-gather = s32[4,1,64]{2,1,0:T(1,128)S(1)} all-gather(s32[1,1,64]{2,1,0:T(1,128)} %bitcast.27), channel_id=1, replica_groups=mesh['fsdp'=4,'ctx'=64] {'fsdp'}, dimensions={0}, use_global_device_ids=true | all-gather | bytes 1280 | tf_op jit(solution)/shard_map/all_gather | solution.py:641
  9.1 0.8 reshape_squeeze.3
  9.9 0.1 reshape.24
  10.0 1.1 copy.17
  11.2 1.1 copy.16
  12.3 0.1 convert_multiply_fusion
  12.4 0.1 reshape.25
  12.5 0.1 reshape.26
  12.6 0.1 pad_maximum_fusion
  12.7 0.0 copy-done.1
  12.7 0.0 copy-done.3
  12.7 0.0 copy-done.4
  12.7 0.0 copy-done.2
  12.7 42.1 %spread.1 = (bf16[64,16,256]{2,1,0:T(8,128)(2,1)S(1)}, bf16[64,16,256]{2,1,0:T(8,128)(2,1)S(1)}, f32[64,1,128]{2,1,0:T(1,128)S(1)}, bf16[64,64,128]{2,1,0:T(8,12...) custom-call(bf16[128,2048]{1,0:T(8,128)(2,1)S(1)} %bitcast.18, ...), custom_call_target="tpu_custom_call" | custom-call | tf_op jit(solution)/shard_map/spread/pallas_call | solution.py:240
  54.8 0.0 copy-start
  54.8 1.3 copy-done
  56.1 34.3 %attn.1 = (f32[64,16,256]{2,1,0:T(8,128)S(1)}, f32[64,64,128]{2,1,0:T(8,128)}) custom-call(s32[2]{0:T(128)S(1)} %pad_add_fusion.geo, s32[64]{0:T(128)S(1)} %dynamic-slice_bitcast_fusion.order, bf16[64,16,256]{2,1,0:T(8,128)(2,1)S(1)} %get-tuple-element.14.q_ref, bf16[64,16,256]{2,1,0:T(8,128)(2,1)S(1)} %get-tuple-element.15.do_ref, ...), custom_call_target="tpu_custom_call" | custom-call | tf_op jit(solution)/shard_map/attn/pallas_call | solution.py:361
  90.4 68.9 %collect.1 = (bf16[128,1024]{1,0:T(8,128)(2,1)S(1)}, bf16[128,2048]{1,0:T(8,128)(2,1)S(1)}, f32[8,512]{1,0:T(8,128)S(1)}) custom-call(f32[64,16,256]{2,1,0:T(8,128)S(1)} %get-tuple-element.18.dq, f32[64,64,128]{2,1,0:T(8,128)} %get-tuple-element.19.dkv, bf16[4,512,512]{2,1,0:T(8,128)(2,1)} %copy-done, bf16[4,128,512]{2,1,0:T(8,128)(2,1)S(1)} %get-tuple-element.21.hid_buf), custom_call_target="tpu_custom_call" | custom-call | tf_op jit(solution)/shard_map/collect/pallas_call | solution.py:598
  159.3 0.7 copy.24
  160.0 0.8 copy.25
  160.8 0.6 copy.26
  (4 shorter events, 0.1 us)
Async XLA Ops:
  0.6 12.1 %copy-start.1 = (bf16[1,128,1024]{2,1,0:T(8,128)(2,1)S(1)}, bf16[1,128,1024]{2,1,0:T(8,128)(2,1)}, u32[]{:S(2)}) copy-start(bf16[1,128,1024]{2,1,0:T(8,128)(2,1)} %param.10) | copy-start | bytes 786436
  0.6 12.0 %copy-start.3 = (bf16[512,512]{1,0:T(8,128)(2,1)S(1)}, bf16[512,512]{1,0:T(8,128)(2,1)}, u32[]{:S(2)}) copy-start(bf16[512,512]{1,0:T(8,128)(2,1)} %w.1) | copy-start | bytes 1572868
  0.7 12.0 %copy-start.4 = (bf16[1,128,1024]{2,1,0:T(8,128)(2,1)S(1)}, bf16[1,128,1024]{2,1,0:T(8,128)(2,1)}, u32[]{:S(2)}) copy-start(bf16[1,128,1024]{2,1,0:T(8,128)(2,1)} %param.8) | copy-start | bytes 786436
  0.7 12.0 %copy-start.2 = (bf16[1,128,2048]{2,1,0:T(8,128)(2,1)S(1)}, bf16[1,128,2048]{2,1,0:T(8,128)(2,1)}, u32[]{:S(2)}) copy-start(bf16[1,128,2048]{2,1,0:T(8,128)(2,1)} %param.7) | copy-start | bytes 1572868
  54.8 1.3 copy-start

commit v2 on v0

v2 whole, which is shorter than its diff:
```python
import functools

import jax
import jax.numpy as jnp
from jax import lax
from jax.experimental import pallas as pl
from jax.experimental.pallas import tpu as pltpu
from jax.sharding import PartitionSpec as P

BF, F32 = jnp.bfloat16, jnp.float32
NT = (((1,), (1,)), ((), ()))
TN = (((0,), (0,)), ((), ()))
MESH = pl.DeviceIdType.MESH
Q_HEADS, KV_HEADS, HEAD_DIM = 16, 4, 64
NX, NZ = 4, 8
VMEM = pl.BlockSpec(memory_space=pltpu.VMEM)


def place():
    f, c = lax.axis_index("fsdp"), lax.axis_index("ctx")
    return c // 16, (c // 2) % 8, c % 2, f // 2, f % 2


def dev(x, z, hi, lo, core):
    return {"fsdp": lo * 2 + core, "ctx": (x * 8 + z) * 2 + hi}


def rcopy(src, dst, send, recv, to):
    return pltpu.make_async_remote_copy(
        src_ref=src, dst_ref=dst, send_sem=send, recv_sem=recv, device_id=to, device_id_type=MESH
    )


def greet(to):
    pl.semaphore_signal(pltpu.get_barrier_semaphore(), inc=1, device_id=to, device_id_type=MESH)

META, W, WF, Q, QF, KV, HID, ZG, ZR, DQS, DQ, KVR, XA, CX, YR, ZW, FIN = (
    0, 1, 4, 6, 9, 12, 14, 16, 32, 48, 49, 50, 51, 55, 59, 63, 70
)
N_SEMS = 71


def backward_kernel(
    hid, w, q, do, stat, meta,
    dq_out, in_out, wg_out,
    meta_rx, order, w_all, acc, kvs, q_buf, do_buf, stat_buf, kv_buf, hid_buf,
    qz, dz, ks, kts, lse, dlt, dqt, dkv, p0, d0, p1, d1,
    dqs, dqs_tx, dqs_rx, dq_tx, rs_tx, rs_rx, finx, kvg, hid_t, wpart, c_rx, ws, y1, y1_rx, y2_rx, wz, wz_rx, wf,
    ssem, rsem,
):
    x, z, hi, lo, core = place()
    f = lo * 2 + core
    sib = dev(x, z, hi, lo, 1 - core)
    near = dev(x, z, hi, 1 - lo, core)
    far = dev(x, z, 1 - hi, 1 - lo, core)
    own = hi == core

    def xdev(i):
        return dev((x + i) % NX, z, hi, lo, core)

    def zdev(i):
        return dev(x, (z + i) % NZ, hi, lo, core)

    def copy(src, dst, sem, to):
        return rcopy(src, dst, ssem.at[sem], rsem.at[sem], to)

    def arrived(ref, sem):
        rcopy(ref, ref, ssem.at[sem], rsem.at[sem], sib).wait_recv()

    low_bit = (hi + lo) % 2
    x_end = hi * 2 + low_bit
    stays = (x == x_end) & own & (x // 2 == lo) & (x % 2 == core)

    for to in [sib, near, far, xdev(1), xdev(3)] + [zdev(i) for i in range(1, NZ)]:
        greet(to)

    def greet_q(i, c):
        greet(dev((x + i // NZ) % NX, (z + i) % NZ, 1 - core, lo, hi))
        return c

    lax.fori_loop(0, 32, greet_q, 0)

    def greet_kv(i, c):
        dx, h = i // 2, i % 2

        @pl.when(jnp.logical_not((dx == 0) & own & (h == hi)))
        def _():
            greet(dev((x + dx) % NX, z, h, lo, hi))

        return c

    lax.fori_loop(0, 8, greet_kv, 0)

    @pl.when(jnp.logical_not(stays))
    def _():
        greet(dev(f, z, x // 2, (x // 2 + x) % 2, hi))

    pl.semaphore_wait(
        pltpu.get_barrier_semaphore(), 12 + 32 + 8 + 1 - own.astype(jnp.int32) - stays.astype(jnp.int32)
    )

    w_own = pltpu.make_async_copy(w, w_all.at[f], ssem.at[N_SEMS])
    w_own.start()
    half = w.shape[0] // 2
    sends = [
        copy(w.at[pl.ds(0, half)], w_all.at[f, pl.ds(0, half)], W, near),
        copy(w.at[pl.ds(half, half)], w_all.at[f, pl.ds(half, half)], W + 1, far),
        copy(w, w_all.at[f], W + 2, sib),
        copy(meta, meta_rx, META, sib),
    ]
    for c in sends:
        c.start()

    slot = hi * 32 + x * 8 + z

    def q_copies(i):
        tx, tz = (x + i // NZ) % NX, (z + i) % NZ
        to = dev(tx, tz, core, lo, 1 - hi)
        rows, cols = pl.ds(pl.multiple_of(tz * 16, 16), 16), pl.ds(pl.multiple_of(tx * 256, 256), 256)
        return (
            copy(q.at[rows, cols], q_buf.at[slot], Q, to),
            copy(do.at[rows, cols], do_buf.at[slot], Q + 1, to),
            copy(stat.at[tx, tz], stat_buf.at[slot], Q + 2, to),
        )

    def send_q(i, c):
        for one in q_copies(i):
            one.start()
        return c

    lax.fori_loop(0, 32, send_q, 0)

    def project(chunk):
        cols = pl.ds(pl.multiple_of(chunk * 512, 512), 512)
        return jnp.dot(hid[:, cols], w_all[chunk], preferred_element_type=F32)

    w_own.wait()
    acc[...] = project(f)
    arrived(w_all.at[0], W + 2)
    acc[...] += project(lo * 2 + 1 - core)
    other, last = (1 - lo) * 2 + core, (1 - lo) * 2 + 1 - core
    for i in range(2):
        part = w_all.at[other, pl.ds(i * half, half)]
        arrived(part, W + i)
        sends.append(copy(part, part, WF + i, sib))
        sends[-1].start()
    acc[...] += project(other)
    for i in range(2):
        arrived(w_all.at[last, pl.ds(i * half, half)], WF + i)
    key_vals = (acc[...] + project(last)).astype(BF)
    for g in range(KV_HEADS):
        kvs[g] = jnp.concatenate(
            [key_vals[:, g * 64 : g * 64 + 64], key_vals[:, 256 + g * 64 : 320 + g * 64]], axis=1
        )

    def to_group(dx, j):
        tx = (x + dx) % NX
        rows, cols = pl.ds(j * 64, 64), pl.ds(pl.multiple_of(tx * 512, 512), 512)
        mine = x * 2 + hi
        return (
            (kvs.at[tx, rows], kv_buf.at[z * 8 + mine], KV + x // 2),
            (hid.at[rows, cols], hid_buf.at[mine], HID),
        ), dev(tx, z, core, lo, j)

    def to_groups(which, act):
        for dx in range(NX):
            for j in range(2):
                pieces, to = to_group(dx, j)
                if dx > 0:
                    act(copy(*pieces[which], to))
                else:
                    mine = own & (core == j)

                    @pl.when(jnp.logical_not(mine))
                    def _():
                        act(copy(*pieces[which], to))

                    @pl.when(mine)
                    def _():
                        src, dst, sem = pieces[which]
                        act(pltpu.make_async_copy(src, dst, rsem.at[sem]))

    def start(c):
        c.start()

    to_groups(0, start)
    to_groups(1, start)

    def z_part(src_z, u):
        return pl.ds(pl.multiple_of(src_z * 8 + u * 4, 4), 4)

    def z_copy(d, s, u):
        part = kv_buf.at[z_part((z + 8 - s) % NZ if d == 0 else (z + s) % NZ, u)]
        return copy(part, part, ZG + (d * 4 + s) * 2 + u, zdev(1) if d == 0 else zdev(7))

    for s in range(4):
        for u in range(2):
            if s == 0:
                arrived(kv_buf.at[pl.ds(0, 4)], KV + u)
            for d in range(2):
                if s == 3 and u != d:
                    continue
                if s:
                    z_copy(d, s - 1, u).wait_recv()
                sends.append(z_copy(d, s, u))
                sends[-1].start()

    got = pl.ds(pl.multiple_of((1 - core) * 32, 32), 32)
    theirs = pl.ds(pl.multiple_of(core * 32, 32), 32)
    bufs = (q_buf, do_buf, stat_buf)
    for i, buf in enumerate(bufs):
        arrived(buf.at[got], Q + i)
        sends.append(copy(buf.at[got], buf.at[got], QF + i, sib))
        sends[-1].start()

    arrived(meta_rx, META)

    @pl.when(own)
    def _():
        c = pltpu.make_async_copy(meta, order, ssem.at[N_SEMS])
        c.start()
        c.wait()

    @pl.when(jnp.logical_not(own))
    def _():
        c = pltpu.make_async_copy(meta_rx, order, ssem.at[N_SEMS])
        c.start()
        c.wait()

    for i, buf in enumerate(bufs):
        arrived(buf.at[theirs], QF + i)

    low = lax.broadcasted_iota(jnp.int32, (16, 128), 1) < 64
    low1 = lax.broadcasted_iota(jnp.int32, (1, 128), 1) < 64

    def sort_q(blk, c):
        stats = []
        for off in range(8):
            b = order[1, blk * 8 + off]
            s = (b % 2) * 32 + b // 2
            for hp in range(2):
                qq = q_buf[s, :, hp * 128 : (hp + 1) * 128].astype(F32) * 0.125
                dd = do_buf[s, :, hp * 128 : (hp + 1) * 128].astype(F32)
                for ho in range(2):
                    rows = slice(off * 64 + hp * 32 + ho * 16, off * 64 + hp * 32 + ho * 16 + 16)
                    qh = qq if ho == 0 else pltpu.roll(qq, 64, 1)
                    dh = dd if ho == 1 else pltpu.roll(dd, 64, 1)
                    qz[blk, rows, :] = jnp.where(low, qh, 0.0).astype(BF)
                    dz[blk, rows, :] = jnp.where(low, 0.0, dh).astype(BF)
            stats.append(stat_buf[s])
        for j in range(4):
            a, b = stats[2 * j], stats[2 * j + 1]
            lse[blk, :, j * 128 : (j + 1) * 128] = jnp.where(low1, a, pltpu.roll(b, 64, 1))
            dlt[blk, :, j * 128 : (j + 1) * 128] = jnp.where(low1, pltpu.roll(a, 64, 1), b)
        dqt[blk] = jnp.zeros((64, 512), F32)
        return c

    lax.fori_loop(0, 8, sort_q, 0)

    for d, s, u in ((0, 2, 1), (1, 2, 0), (0, 3, 0), (1, 3, 1)):
        z_copy(d, s, u).wait_recv()

    def sort_kv(blk, c):
        for off in range(8):
            b = order[1, blk * 8 + off]
            ks[blk, off * 64 : off * 64 + 64, :] = kv_buf[((b // 2) % 8) * 8 + (b // 16) * 2 + b % 2]
        kts[blk] = ks[blk].astype(F32).T[:64].astype(BF)
        return c

    lax.fori_loop(0, 8, sort_kv, 0)

    def probs(m, c, pb, db, diag):
        for a in range(2):
            keys = slice(a * 256, (a + 1) * 256)
            kv = ks[m, keys, :]
            first = a * 256 if diag else 0
            qs = slice(first, 512)
            n = 512 - first
            p = jnp.exp(lax.dot_general(kv, qz[c, qs], NT, preferred_element_type=F32) - lse[c, :, qs])
            if diag:
                kp = lax.broadcasted_iota(jnp.int32, (256, n), 0) + a * 256
                qp = lax.broadcasted_iota(jnp.int32, (256, n), 1) + first
                kpos = (kp // 64) * 128 + (kp % 64) + core * 64
                qpos = (qp // 64) * 128 + (qp % 16) + z * 16
                p = jnp.where(kpos <= qpos, p, 0.0)
            dp = lax.dot_general(kv, dz[c, qs], NT, preferred_element_type=F32)
            db[keys, qs] = (p * (dp - dlt[c, :, qs])).astype(BF)
            pb[keys, qs] = p.astype(BF)

    def dot(a, b):
        return jnp.dot(a, b, preferred_element_type=F32)

    def diag_grads(m, pb, db):
        top = dot(db[:256, :], qz[m]) + dot(pb[:256, :], dz[m])
        bottom = dot(db[256:, 256:], qz[m, 256:]) + dot(pb[256:, 256:], dz[m, 256:])
        dkv[pl.ds(m * 8, 4)] = top.reshape(4, 64, 128)
        dkv[pl.ds(m * 8 + 4, 4)] = bottom.reshape(4, 64, 128)
        dqt[m, :, :256] += dot(kts[m, :, :256], db[:256, :256])
        dqt[m, :, 256:] += dot(kts[m], db[:, 256:])

    def grads(m, c, pb, db):
        ds, p = db[...], pb[...]
        dkv[pl.ds(m * 8, 8)] += (dot(ds, qz[c]) + dot(p, dz[c])).reshape(8, 64, 128)
        dqt[c] += dot(kts[m], ds)

    def diagonal(i, c):
        probs(2 * i, 2 * i, p0, d0, True)
        probs(2 * i + 1, 2 * i + 1, p1, d1, True)
        diag_grads(2 * i, p0, d0)
        diag_grads(2 * i + 1, p1, d1)
        return c

    lax.fori_loop(0, 4, diagonal, 0)

    def following(m, c):
        wrap = c == 7
        return jnp.where(wrap, m + 1, m), jnp.where(wrap, jnp.minimum(m + 2, 7), c + 1)

    def below(i, carry):
        m, c = carry
        m1, c1 = following(m, c)
        probs(m, c, p0, d0, False)
        probs(m1, c1, p1, d1, False)
        grads(m, c, p0, d0)
        grads(m1, c1, p1, d1)
        return following(m1, c1)

    lax.fori_loop(0, 14, below, (0, 1))

    def r_copy(d, s, u):
        return copy(
            rs_tx.at[d, s, u], rs_rx.at[d, s, u], ZR + (d * 4 + s) * 2 + u, zdev(1) if d == 0 else zdev(7)
        )

    def terms(tz, u):
        parts = []
        for i in range(4):
            b = ((u * 2 + i // 2) * 8 + tz) * 2 + i % 2
            parts.append(dkv[order[0, b]][None])
        return jnp.concatenate(parts, axis=0)

    def r_step(s):
        for u in range(2):
            for d in range(2):
                if s == 0 and u != d:
                    continue
                t = terms((z + 4 - s) % NZ if d == 0 else (z + 4 + s) % NZ, u)
                if s > 1 or (s == 1 and u == d):
                    r_copy(d, s - 1, u).wait_recv()
                    t = t + rs_rx[d, s - 1, u].astype(F32)
                rs_tx[d, s, u] = t.astype(BF)
                sends.append(r_copy(d, s, u))
                sends[-1].start()

    r_step(0)

    def place_q(blk, c):
        for j in range(4):
            t = (dqt[blk, :, j * 128 : (j + 1) * 128] * 0.125).T
            for o in range(2):
                dqs[blk * 8 + j * 2 + o] = jnp.concatenate(
                    [t[o * 64 + h * 16 : o * 64 + h * 16 + 16] for h in range(4)], axis=1
                )
        return c

    lax.fori_loop(0, 8, place_q, 0)
    r_step(1)

    def give_q(i, c):
        for j in range(4):
            k = i * 4 + j
            dqs_tx[k] = dqs[order[0, k * 2 + core]]
        return c

    lax.fori_loop(0, 8, give_q, 0)
    sends.append(copy(dqs_tx, dqs_rx, DQS, sib))
    sends[-1].start()
    r_step(2)

    arrived(hid_buf, HID)
    for i in range(4):
        cols = slice(i * 128, (i + 1) * 128)
        hid_t[cols, :] = hid_buf[:, :, cols].reshape(512, 128).astype(F32).T.astype(BF)
    r_step(3)

    for u in range(2):
        t = terms(z, u)
        for d in range(2):
            r_copy(d, 3, u).wait_recv()
            t = t + rs_rx[d, 3, u].astype(F32)
        finx[x, u * 4 : u * 4 + 4] = t.astype(BF)

    def x_copy(i):
        src = (x + (0, 0, 3, 1)[i]) % NX
        part = finx.at[src] if i < 2 else finx.at[src, pl.ds((i - 2) * 4, 4)]
        return copy(part, part, XA + i, xdev((1, 3, 1, 3)[i]))

    for i in range(2):
        sends.append(x_copy(i))
        sends[-1].start()

    krows = pl.ds(pl.multiple_of(core * 64, 64), 64)

    def to_owners(act):
        for dx in range(NX):
            for h in range(2):
                tx = (x + dx) % NX
                src, dst = finx.at[x, tx * 2 + h], kvg.at[x, krows]
                if dx > 0:
                    act(copy(src, dst, KVR, dev(tx, z, h, lo, hi)))
                else:
                    mine = own & (hi == h)

                    @pl.when(jnp.logical_not(mine))
                    def _():
                        act(copy(src, dst, KVR, dev(tx, z, h, lo, hi)))

                    @pl.when(mine)
                    def _():
                        act(pltpu.make_async_copy(src, dst, rsem.at[KVR]))

    to_owners(start)

    arrived(dqs_rx, DQS)

    def add_q(i, c):
        for j in range(4):
            k = i * 4 + j
            dq_tx[k] = (dqs[order[0, k * 2 + 1 - core]] + dqs_rx[k]).astype(BF)
        return c

    lax.fori_loop(0, 8, add_q, 0)
    rows, cols = pl.ds(pl.multiple_of(z * 16, 16), 16), pl.ds(pl.multiple_of(x * 256, 256), 256)

    def q_return(i):
        tx, tz = (x + i // NZ) % NX, (z + i) % NZ
        return copy(dq_tx.at[tx * 8 + tz], dq_out.at[rows, cols], DQ, dev(tx, tz, 1 - core, lo, hi))

    def return_q(i, c):
        q_return(i).start()
        return c

    lax.fori_loop(0, 32, return_q, 0)

    def c_copy(i):
        g = (x + i) % NX
        return copy(wpart.at[1 - core, g], c_rx.at[g], CX + i, sib)

    def grad_w(i):
        g = (x + i) % NX
        r = dot(hid_t[...], finx[g].reshape(512, 128)).reshape(32, 2, 8, 128)
        for c in range(2):
            wpart[c, g] = r[:, c].reshape(256, 128)
        sends.append(c_copy(i))
        sends[-1].start()

    grad_w(0)
    for i in range(2):
        x_copy(i).wait_recv()
        sends.append(x_copy(2 + i))
        sends[-1].start()
    grad_w(3)
    grad_w(1)
    for i in range(2):
        x_copy(2 + i).wait_recv()
    grad_w(2)

    for i in (0, 3, 1, 2):
        g = (x + i) % NX
        c_copy(i).wait_recv()
        ws[g] = (wpart[core, g] + c_rx[g]).reshape(2, 2, 64, 128)

    def y_first(i):
        if i == 0:
            return copy(ws.at[pl.ds(0, 2), :, 1 - low_bit], y1_rx.at[0], YR, near)
        return copy(ws.at[pl.ds(2, 2), 1 - hi], y1_rx.at[1], YR + 1, far)

    def y_second(i):
        return copy(y1.at[i, :, 1 - (low_bit if i else hi)], y2_rx.at[i], YR + 2 + i, near if i else far)

    for i in range(2):
        sends.append(y_first(i))
        sends[-1].start()

    arrived(kvg, KVR)
    kvn = jnp.concatenate([kvg[g, :, :64] for g in range(4)] + [kvg[g, :, 64:] for g in range(4)], axis=1)
    for i in range(4):
        in_out[:, i * 512 : (i + 1) * 512] = lax.dot_general(
            kvn, w_all[i], NT, preferred_element_type=F32
        ).astype(BF)

    for i in range(2):
        y_first(i).wait_recv()
        for g in range(2):
            for k in range(2):
                kept = ws[g, k, low_bit] if i == 0 else ws[2 + g, hi, k]
                y1[i, g, k] = kept + y1_rx[i, g, k]
        sends.append(y_second(i))
        sends[-1].start()
    for i in range(2):
        y_second(i).wait_recv()
        for g in range(2):
            wz[i * 2 + g] = y1[i, g, low_bit if i else hi] + y2_rx[i, g]

    def z_rows(tz):
        return pl.ds(pl.multiple_of(tz * 8, 8), 8)

    def zw_copy(i):
        return copy(wz.at[:, z_rows((z + i) % NZ)], wz_rx.at[i - 1], ZW + i - 1, zdev(i))

    for i in range(1, NZ):
        sends.append(zw_copy(i))
        sends[-1].start()
    total = wz[:, z_rows(z)]
    for i in range(1, NZ):
        zw_copy(i).wait_recv()
        total = total + wz_rx[i - 1]
    wf[...] = jnp.concatenate([total[g, :, :64] for g in range(4)] + [total[g, :, 64:] for g in range(4)], axis=1)

    end = copy(wf, wg_out, FIN, dev(x_end, z, core, x // 2, x % 2))

    @pl.when(jnp.logical_not(stays))
    def _():
        end.start()

    @pl.when(stays)
    def _():
        pltpu.make_async_copy(wf, wg_out, rsem.at[FIN]).start()

    arrived(wg_out, FIN)
    arrived(dq_tx, DQ)
    for c in sends:
        c.wait_send()

    def done_q(i, c):
        for one in q_copies(i):
            one.wait_send()
        q_return(i).wait_send()
        return c

    lax.fori_loop(0, 32, done_q, 0)

    def sent(c):
        if c.is_remote:
            c.wait_send()

    to_groups(0, sent)
    to_groups(1, sent)
    to_owners(sent)

    @pl.when(jnp.logical_not(stays))
    def _():
        end.wait_send()


def backward(hid, w, q, do, stat, meta):
    v = pltpu.VMEM
    return pl.pallas_call(
        backward_kernel,
        name="backward",
        out_shape=(
            jax.ShapeDtypeStruct((128, 1024), BF),
            jax.ShapeDtypeStruct((128, 2048), BF),
            jax.ShapeDtypeStruct((8, 512), F32),
        ),
        in_specs=[VMEM] * 6,
        out_specs=[VMEM] * 3,
        scratch_shapes=[
            v((8, 128), jnp.int32),
            pltpu.SMEM((8, 128), jnp.int32),
            v((4, 512, 512), BF),
            v((128, 512), F32),
            v((4, 128, 128), BF),
            v((64, 16, 256), BF),
            v((64, 16, 256), BF),
            v((64, 1, 128), F32),
            v((64, 64, 128), BF),
            v((8, 64, 512), BF),
            v((8, 512, 128), BF),
            v((8, 512, 128), BF),
            v((8, 512, 128), BF),
            v((8, 64, 512), BF),
            v((8, 1, 512), F32),
            v((8, 1, 512), F32),
            v((8, 64, 512), F32),
            v((64, 64, 128), F32),
            v((512, 512), BF),
            v((512, 512), BF),
            v((512, 512), BF),
            v((512, 512), BF),
            v((64, 16, 256), F32),
            v((32, 16, 256), F32),
            v((32, 16, 256), F32),
            v((32, 16, 256), BF),
            v((2, 4, 2, 4, 64, 128), BF),
            v((2, 4, 2, 4, 64, 128), BF),
            v((4, 8, 64, 128), BF),
            v((4, 128, 128), BF),
            v((512, 512), BF),
            v((2, 4, 256, 128), F32),
            v((4, 256, 128), F32),
            v((4, 2, 2, 64, 128), F32),
            v((2, 2, 2, 64, 128), F32),
            v((2, 2, 2, 64, 128), F32),
            v((2, 2, 64, 128), F32),
            v((4, 64, 128), F32),
            v((7, 4, 8, 128), F32),
            v((8, 512), F32),
            pltpu.SemaphoreType.DMA((N_SEMS + 1,)),
            pltpu.SemaphoreType.DMA((N_SEMS,)),
        ],
        compiler_params=pltpu.CompilerParams(
            collective_id=0, has_side_effects=True, vmem_limit_bytes=56 * 2**20
        ),
    )(hid, w, q, do, stat, meta)


def shards(hidden, queries, attn_out, grad_out, log_sums, block_order, w_kv):
    delta = jnp.sum(
        (grad_out[0].astype(F32) * attn_out[0].astype(F32)).reshape(128, Q_HEADS, HEAD_DIM), axis=2
    ).T

    def sliced(a):
        return a.reshape(4, 4, 8, 16).transpose(0, 2, 1, 3).reshape(4, 8, 64)

    stat = jnp.concatenate([sliced(log_sums[0]), sliced(delta)], axis=2).reshape(4, 8, 1, 128)
    ids = lax.broadcasted_iota(jnp.int32, (64, 64), 1)
    there = block_order[0][None, :] == lax.broadcasted_iota(jnp.int32, (64, 64), 0)
    back = jnp.sum(jnp.where(there, ids, 0), axis=1)
    meta = jnp.pad(jnp.stack([block_order[0], back]), ((0, 6), (0, 64)))
    dq_out, in_out, wg = backward(hidden[0], w_kv, queries[0], grad_out[0], stat, meta)
    return dq_out[None], in_out[None], wg


def solution(mesh):
    return jax.shard_map(
        shards,
        mesh=mesh,
        in_specs=(
            P("fsdp", "ctx", None),
            P("fsdp", "ctx", None),
            P("fsdp", "ctx", None),
            P("fsdp", "ctx", None),
            P("fsdp", None, "ctx"),
            P("fsdp", None),
            P("fsdp", None),
        ),
        out_specs=(P("fsdp", "ctx", None), P("fsdp", "ctx", None), P(("fsdp", "ctx"), None)),
        check_vma=False,
    )
```

time: 2450 us -> 131 us (0.05)
  waiting for transfers between devices: 2180 us -> 0 us
  Pallas kernels: 0 us -> 123 us
  loops' own time: 87.9 us -> 0 us
  matrix products: 85 us -> 0 us
  local copies, waits for them, and re-layouts: 53.3 us -> 5.22 us
    unnamed x3 -> x0, waiting for transfers between devices: 1410 us -> none
    ppermute x127 -> x0, waiting for transfers between devices: 736 us -> none  [shifted(): lax.ppermute(array, axis, [(i, (i + by) % size) for i in range(size)])]
    pallas_call x0 -> x1, Pallas kernels: none -> 123 us  [backward(): pl.pallas_call(backward_kernel, name='backward', out_shape=(jax.ShapeDtyp...]
    another operation x64 -> x0, loops' own time: 87.9 us -> none  [the longest x1 86 us: shards(): lax.fori_loop(1, ahead + 1, ahead_step, (key_vals, own_keys, own_query))]
    dot_general x258 -> x0, matrix products: 85 us -> none  [the longest x51 18 us: block_grads(): jnp.einsum('qgnd,kgd->gnqk', query4, key4, preferred_element_type=jnp.flo...]
    dynamic_slice x64 -> x0, local copies, waits for them, and re-layouts: 41.6 us -> none  [the longest x63 41 us: ahead_step(): order_row[(position - hop_index) % cycle_size]]
    all_gather x1 -> x0, waiting for transfers between devices: 33.7 us -> none  [shards(): w_all = lax.all_gather(w_kv, 'fsdp', axis=0, tiled=True)]
  transfers between devices with their start and end apart: 129 -> 0, of which waited for: 66 -> 0; matrix products, arithmetic and copies ran while one was open for 5% -> 0% of each run, Pallas kernels for 0% -> 0%
where the time goes in v2:
time: 131 us
  Pallas kernels  123 us (94%)
  local copies, waits for them, and re-layouts  5.22 us (4%)
  other arithmetic  2.26 us (2%)
    pallas_call x1, Pallas kernels, backward(): pl.pallas_call(backward_kernel, name='backward', out_shape=(jax.ShapeDtyp...  123 us
    unnamed x15, local copies, waits for them, and re-layouts  4.25 us

profile of v2, /device:TPU:1, one launch (start us, length us, event | category | flops | bytes accessed | tf_op | source)
XLA Modules:
  0.0 130.9 jit_solution(5046130036831538465)
XLA Ops:
  0.6 0.0 copy-start.4
  0.6 0.0 copy-start.2
  0.7 0.8 select_reduce_fusion
  1.5 0.7 pad_add_fusion
  2.1 0.6 pad.4.meta
  2.7 0.0 copy-done.4
  2.7 0.1 reshape_squeeze.3
  2.8 0.1 reshape.24
  2.9 0.0 copy-done.2
  2.9 0.0 copy-start
  3.0 0.2 copy.17
  3.1 0.8 copy-done
  3.9 0.2 copy.16
  4.1 0.1 convert_multiply_fusion
  4.2 0.1 reshape.25
  4.3 0.1 reshape.26
  4.4 0.7 pad_maximum_fusion
  5.1 122.7 %backward.1 = (bf16[128,1024]{1,0:T(8,128)(2,1)}, bf16[128,2048]{1,0:T(8,128)(2,1)}, f32[8,512]{1,0:T(8,128)}) custom-call(bf16[128,2048]{1,0:T(8,128)(2,1)} %bitcast.16, bf16[512,512]{1,0:T(8,128)(2,1)} %w.1, bf16[128,1024]{1,0:T(8,128)(2,1)} %bitcast.18, bf16[128,1024]{1,0:T(8,128)(2,1)} %bitcast.15, f32[4,8,1,128]{3,2,1,0:T(1,128)} %bitcast.22, ...), custom_call_target="tpu_custom_call" | custom-call | tf_op jit(solution)/shard_map/backward/pallas_call | solution.py:558
  127.8 0.0 copy-start.1
  127.8 1.7 %copy.24 = bf16[1,128,1024]{2,1,0:T(8,128)(2,1)} copy(bf16[1,128,1024]{2,1,0:T(8,128)(2,1)} %bitcast.20) | data formatting | bytes 524288
  129.5 0.0 copy-done.1
  129.5 0.0 copy-start.3
  129.5 0.8 copy.25
  130.3 0.0 copy-done.3
  130.3 0.6 copy.26
  (3 shorter events, 0.1 us)
Async XLA Ops:
  0.6 2.1 %copy-start.4 = (f32[1,16,128]{2,1,0:T(8,128)S(1)}, f32[1,16,128]{2,1,0:T(8,128)}, u32[]{:S(2)}) copy-start(f32[1,16,128]{2,1,0:T(8,128)} %param.11) | copy-start | bytes 24580
  0.6 2.3 %copy-start.2 = (bf16[1,128,1024]{2,1,0:T(8,128)(2,1)S(1)}, bf16[1,128,1024]{2,1,0:T(8,128)(2,1)}, u32[]{:S(2)}) copy-start(bf16[1,128,1024]{2,1,0:T(8,128)(2,1)} %param.9) | copy-start | bytes 786436
  2.9 1.0 copy-start
  127.8 1.7 %copy-start.1 = (bf16[128,2048]{1,0:T(8,128)(2,1)S(1)}, bf16[128,2048]{1,0:T(8,128)(2,1)}, u32[]{:S(2)}) copy-start(bf16[128,2048]{1,0:T(8,128)(2,1)} %get-tuple-element.7) | copy-start | bytes 1572868
  129.5 0.8 copy-start.3

commit v3 on v2

v3 whole, which is shorter than its diff:
```python
import functools

import jax
import jax.numpy as jnp
from jax import lax
from jax.experimental import pallas as pl
from jax.experimental.pallas import tpu as pltpu
from jax.sharding import PartitionSpec as P

BF, F32 = jnp.bfloat16, jnp.float32
NT = (((1,), (1,)), ((), ()))
TN = (((0,), (0,)), ((), ()))
MESH = pl.DeviceIdType.MESH
Q_HEADS, KV_HEADS, HEAD_DIM = 16, 4, 64
NX, NZ = 4, 8
VMEM = pl.BlockSpec(memory_space=pltpu.VMEM)


def place():
    f, c = lax.axis_index("fsdp"), lax.axis_index("ctx")
    return c // 16, (c // 2) % 8, c % 2, f // 2, f % 2


def dev(x, z, hi, lo, core):
    return {"fsdp": lo * 2 + core, "ctx": (x * 8 + z) * 2 + hi}


def rcopy(src, dst, send, recv, to):
    return pltpu.make_async_remote_copy(
        src_ref=src, dst_ref=dst, send_sem=send, recv_sem=recv, device_id=to, device_id_type=MESH
    )


def greet(to):
    pl.semaphore_signal(pltpu.get_barrier_semaphore(), inc=1, device_id=to, device_id_type=MESH)

META, W, WF, Q, QF, KV, HID, ZG, ZR, DQS, DQ, KVR, XA, CX, WR = (
    0, 1, 4, 6, 9, 12, 16, 17, 49, 81, 82, 83, 85, 93, 97
)
N_SEMS = 98
HALF = 32


def backward_kernel(
    hid, w, q, do, stat, mine_order,
    dq_out, in_out, wg_out,
    sib_order, stored_vm, sorted_vm, stored, sorted_, w_all, acc, kvs, q_buf, do_buf, stat_buf, kv_buf0, kv_buf1, hid_buf,
    qz, dz, ks, kts, lse, dlt, dqt, dkv, pbufs, dbufs,
    dqs, dqs_tx, dqs_rx, dq_tx, d_tx, d_rx, rs_tx, rs_rx, finx, kvg, hid_t, wpart, c_rx, w_tx, w_rx,
    ssem, rsem,
):
    x, z, hi, lo, core = place()
    f = lo * 2 + core
    sib = dev(x, z, hi, lo, 1 - core)
    near = dev(x, z, hi, 1 - lo, core)
    far = dev(x, z, 1 - hi, 1 - lo, core)
    own = hi == core

    def xdev(i):
        return dev((x + i) % NX, z, hi, lo, core)

    def zdev(i):
        return dev(x, (z + i) % NZ, hi, lo, core)

    def copy(src, dst, sem, to):
        return rcopy(src, dst, ssem.at[sem], rsem.at[sem], to)

    def arrived(ref, sem):
        rcopy(ref, ref, ssem.at[sem], rsem.at[sem], sib).wait_recv()

    for to in [sib, near, far, xdev(1), xdev(3)] + [zdev(i) for i in range(1, NZ)]:
        greet(to)

    def greet_q(i, c):
        greet(dev((x + i // NZ) % NX, (z + i) % NZ, 1 - core, lo, hi))
        return c

    lax.fori_loop(0, 32, greet_q, 0)

    def greet_kv(i, c):
        dx, h = i // 2, i % 2

        @pl.when(jnp.logical_not((dx == 0) & own & (h == hi)))
        def _():
            greet(dev((x + dx) % NX, z, h, lo, hi))

        return c

    lax.fori_loop(0, 8, greet_kv, 0)

    stays = own & (x // 2 == lo) & (x % 2 == core)

    def w_from(i):
        return dev(f, (z + i) % NZ, (hi + i // 16) % 2, (lo + i // 8) % 2, hi)

    def w_to(i):
        return dev((x + i // NZ) % NX, (z + i) % NZ, core, x // 2, x % 2)

    def greet_w(i, c):
        @pl.when(jnp.logical_not(stays & (i == 0)))
        def _():
            greet(w_from(i))

        return c

    lax.fori_loop(0, 32, greet_w, 0)
    pl.semaphore_wait(
        pltpu.get_barrier_semaphore(), 12 + 32 + 8 + 32 - own.astype(jnp.int32) - stays.astype(jnp.int32)
    )

    w_own = pltpu.make_async_copy(w, w_all.at[f], ssem.at[N_SEMS])
    w_own.start()
    half = w.shape[0] // 2
    sends = [
        copy(w.at[pl.ds(0, half)], w_all.at[f, pl.ds(0, half)], W, near),
        copy(w.at[pl.ds(half, half)], w_all.at[f, pl.ds(half, half)], W + 1, far),
        copy(w, w_all.at[f], W + 2, sib),
        copy(mine_order, sib_order, META, sib),
    ]
    for c in sends:
        c.start()

    slot = hi * 32 + x * 8 + z

    def q_copies(i):
        tx, tz = (x + i // NZ) % NX, (z + i) % NZ
        to = dev(tx, tz, core, lo, 1 - hi)
        rows, cols = pl.ds(pl.multiple_of(tz * 16, 16), 16), pl.ds(pl.multiple_of(tx * 256, 256), 256)
        return (
            copy(q.at[rows, cols], q_buf.at[slot], Q, to),
            copy(do.at[rows, cols], do_buf.at[slot], Q + 1, to),
            copy(stat.at[tx, tz], stat_buf.at[slot], Q + 2, to),
        )

    def send_q(i, c):
        for one in q_copies(i):
            one.start()
        return c

    lax.fori_loop(0, 32, send_q, 0)

    def project(chunk):
        cols = pl.ds(pl.multiple_of(chunk * 512, 512), 512)
        return jnp.dot(hid[:, cols], w_all[chunk], preferred_element_type=F32)

    w_own.wait()
    acc[...] = project(f)
    arrived(w_all.at[0], W + 2)
    acc[...] += project(lo * 2 + 1 - core)
    other, last = (1 - lo) * 2 + core, (1 - lo) * 2 + 1 - core
    for i in range(2):
        part = w_all.at[other, pl.ds(i * half, half)]
        arrived(part, W + i)
        sends.append(copy(part, part, WF + i, sib))
        sends[-1].start()
    acc[...] += project(other)
    for i in range(2):
        arrived(w_all.at[last, pl.ds(i * half, half)], WF + i)
    key_vals = (acc[...] + project(last)).astype(BF)
    for g in range(KV_HEADS):
        kvs[g] = jnp.concatenate(
            [key_vals[:, g * 64 : g * 64 + 64], key_vals[:, 256 + g * 64 : 320 + g * 64]], axis=1
        )

    kv_buf = (kv_buf0, kv_buf1)

    def to_group(dx, j, which):
        tx = (x + dx) % NX
        to = dev(tx, z, core, lo, j)
        mine = x * 2 + hi
        if which < 2:
            rows = pl.ds(j * 64 + which * HALF, HALF)
            return (kvs.at[tx, rows], kv_buf[which].at[z * 8 + mine], KV + which * 2 + x // 2), to
        rows, cols = pl.ds(j * 64, 64), pl.ds(pl.multiple_of(tx * 512, 512), 512)
        return (hid.at[rows, cols], hid_buf.at[mine], HID), to

    def to_groups(which, act):
        for dx in range(NX):
            for j in range(2):
                piece, to = to_group(dx, j, which)
                if dx > 0:
                    act(copy(*piece, to))
                else:
                    mine = own & (core == j)

                    @pl.when(jnp.logical_not(mine))
                    def _():
                        act(copy(*piece, to))

                    @pl.when(mine)
                    def _():
                        src, dst, sem = piece
                        act(pltpu.make_async_copy(src, dst, rsem.at[sem]))

    def start(c):
        c.start()

    to_groups(0, start)
    to_groups(1, start)

    def z_part(src_z, u):
        return pl.ds(pl.multiple_of(src_z * 8 + u * 4, 4), 4)

    def z_copy(e, d, s, u):
        part = kv_buf[e].at[z_part((z + 8 - s) % NZ if d == 0 else (z + s) % NZ, u)]
        return copy(part, part, ZG + e * 16 + (d * 4 + s) * 2 + u, zdev(1) if d == 0 else zdev(7))

    def z_step(e, s):
        for u in range(2):
            if s == 0:
                arrived(kv_buf[e].at[pl.ds(0, 4)], KV + e * 2 + u)
            for d in range(2):
                if s == 3 and u != d:
                    continue
                if s:
                    z_copy(e, d, s - 1, u).wait_recv()
                sends.append(z_copy(e, d, s, u))
                sends[-1].start()

    def z_end(e):
        for d, s, u in ((0, 2, 1), (1, 2, 0), (0, 3, 0), (1, 3, 1)):
            z_copy(e, d, s, u).wait_recv()

    z_step(0, 0)
    z_step(0, 1)
    z_step(1, 0)
    z_step(0, 2)
    z_step(0, 3)
    z_step(1, 1)

    got = pl.ds(pl.multiple_of((1 - core) * 32, 32), 32)
    theirs = pl.ds(pl.multiple_of(core * 32, 32), 32)
    bufs = (q_buf, do_buf, stat_buf)
    for i, buf in enumerate(bufs):
        arrived(buf.at[got], Q + i)
        sends.append(copy(buf.at[got], buf.at[got], QF + i, sib))
        sends[-1].start()

    arrived(sib_order, META)
    there = jnp.where(own, mine_order[...], sib_order[...])
    ids = lax.broadcasted_iota(jnp.int32, (64, 64), 1)
    back = jnp.max(jnp.where(there == lax.broadcasted_iota(jnp.int32, (64, 64), 0), ids, 0), axis=1, keepdims=True)
    stored_vm[...] = there
    sorted_vm[...] = jnp.broadcast_to(back, (64, 128))
    for vm, sm in ((stored_vm, stored), (sorted_vm, sorted_)):
        c = pltpu.make_async_copy(vm, sm, ssem.at[N_SEMS])
        c.start()
        c.wait()

    for i, buf in enumerate(bufs):
        arrived(buf.at[theirs], QF + i)

    low = lax.broadcasted_iota(jnp.int32, (16, 128), 1) < 64
    low1 = lax.broadcasted_iota(jnp.int32, (1, 128), 1) < 64

    def sort_q(blk, c):
        stats = []
        for off in range(8):
            b = sorted_[blk * 8 + off, 0]
            s = (b % 2) * 32 + b // 2
            for hp in range(2):
                qq = q_buf[s, :, hp * 128 : (hp + 1) * 128].astype(F32) * 0.125
                dd = do_buf[s, :, hp * 128 : (hp + 1) * 128].astype(F32)
                for ho in range(2):
                    rows = slice(off * 64 + hp * 32 + ho * 16, off * 64 + hp * 32 + ho * 16 + 16)
                    qh = qq if ho == 0 else pltpu.roll(qq, 64, 1)
                    dh = dd if ho == 1 else pltpu.roll(dd, 64, 1)
                    qz[blk, rows, :] = jnp.where(low, qh, 0.0).astype(BF)
                    dz[blk, rows, :] = jnp.where(low, 0.0, dh).astype(BF)
            stats.append(stat_buf[s])
        for j in range(4):
            a, b = stats[2 * j], stats[2 * j + 1]
            lse[blk, :, j * 128 : (j + 1) * 128] = jnp.where(low1, a, pltpu.roll(b, 64, 1))
            dlt[blk, :, j * 128 : (j + 1) * 128] = jnp.where(low1, pltpu.roll(a, 64, 1), b)
        dqt[blk] = jnp.zeros((64, 512), F32)
        return c

    lax.fori_loop(0, 8, sort_q, 0)

    def sort_kv(e):
        def one(blk, c):
            for off in range(8):
                b = sorted_[blk * 8 + off, 0]
                ks[blk, off * HALF : (off + 1) * HALF, :] = kv_buf[e][((b // 2) % 8) * 8 + (b // 16) * 2 + b % 2]
            kts[blk] = ks[blk].astype(F32).T[:64].astype(BF)
            return c

        lax.fori_loop(0, 8, one, 0)

    def probs(m, c, t, e=None):
        for n, qs in ((256, slice(0, 512)),) if e is None else ((128, slice(0, 256)), (256, slice(256, 512))):
            keys = slice(0, n)
            kv = ks[m, keys, :]
            p = jnp.exp(lax.dot_general(kv, qz[c, qs], NT, preferred_element_type=F32) - lse[c, :, qs])
            if e is not None:
                kp = lax.broadcasted_iota(jnp.int32, p.shape, 0)
                qp = lax.broadcasted_iota(jnp.int32, p.shape, 1) + qs.start
                kpos = (kp // HALF) * 128 + (kp % HALF) + core * 64 + e * HALF
                qpos = (qp // 64) * 128 + (qp % 16) + z * 16
                p = jnp.where(kpos <= qpos, p, 0.0)
            dp = lax.dot_general(kv, dz[c, qs], NT, preferred_element_type=F32)
            dbufs[t, keys, qs] = (p * (dp - dlt[c, :, qs])).astype(BF)
            pbufs[t, keys, qs] = p.astype(BF)

    def dot(a, b):
        return jnp.dot(a, b, preferred_element_type=F32)

    def diag_grads(e, m, t):
        top = dot(dbufs[t, :128, :], qz[m]) + dot(pbufs[t, :128, :], dz[m])
        bottom = dot(dbufs[t, 128:, 256:], qz[m, 256:]) + dot(pbufs[t, 128:, 256:], dz[m, 256:])
        dkv[e, pl.ds(m * 8, 4)] = top.reshape(4, HALF, 128)
        dkv[e, pl.ds(m * 8 + 4, 4)] = bottom.reshape(4, HALF, 128)
        dqt[m, :, :256] += dot(kts[m, :, :128], dbufs[t, :128, :256])
        dqt[m, :, 256:] += dot(kts[m], dbufs[t, :, 256:])

    def grads(e, m, c, t):
        ds, p = dbufs[t], pbufs[t]
        dkv[e, pl.ds(m * 8, 8)] += (dot(ds, qz[c]) + dot(p, dz[c])).reshape(8, HALF, 128)
        dqt[c] += dot(kts[m], ds)

    def diagonal(e):
        def one(i, c):
            for t in range(4):
                probs(4 * i + t, 4 * i + t, t, e)
            for t in range(4):
                diag_grads(e, 4 * i + t, t)
            return c

        lax.fori_loop(0, 2, one, 0)

    def following(m, c):
        wrap = c == 7
        return jnp.where(wrap, m + 1, m), jnp.where(wrap, jnp.minimum(m + 2, 7), c + 1)

    def below(e, n, at):
        def four(i, at):
            tiles = [at]
            for t in range(4):
                probs(*tiles[t], t)
                tiles.append(following(*tiles[t]))
            for t in range(4):
                grads(e, *tiles[t], t)
            return tiles[4]

        return lax.fori_loop(0, n, four, at)

    def r_copy(d, s, u):
        return copy(
            rs_tx.at[d, s, u], rs_rx.at[d, s, u], ZR + 16 + (d * 4 + s) * 2 + u, zdev(1) if d == 0 else zdev(7)
        )

    def terms(e, tz, u):
        parts = []
        for i in range(4):
            b = ((u * 2 + i // 2) * 8 + tz) * 2 + i % 2
            parts.append(dkv[e, stored[0, b]][None])
        return jnp.concatenate(parts, axis=0)

    def r_step(s):
        for u in range(2):
            for d in range(2):
                if s == 0 and u != d:
                    continue
                t = terms(1, (z + 4 - s) % NZ if d == 0 else (z + 4 + s) % NZ, u)
                if s > 1 or (s == 1 and u == d):
                    r_copy(d, s - 1, u).wait_recv()
                    t = t + rs_rx[d, s - 1, u].astype(F32)
                rs_tx[d, s, u] = t.astype(BF)
                sends.append(r_copy(d, s, u))
                sends[-1].start()

    def d_copy(i):
        return copy(d_tx.at[i - 1], d_rx.at[i - 1], ZR + i, zdev(i))

    def d_send():
        for i in (4, 3, 5, 2, 6, 1, 7):
            for u in range(2):
                d_tx[i - 1, u * 4 : u * 4 + 4] = terms(0, (z + i) % NZ, u).astype(BF)
            sends.append(d_copy(i))
            sends[-1].start()

    def x_copy(e, i):
        src = (x + (0, 0, 3, 1)[i]) % NX
        part = finx.at[e, src] if i < 2 else finx.at[e, src, pl.ds((i - 2) * 4, 4)]
        return copy(part, part, XA + e * 4 + i, xdev((1, 3, 1, 3)[i]))

    def to_owners(e, act):
        rows = pl.ds(pl.multiple_of(core * 64 + e * HALF, HALF), HALF)
        for dx in range(NX):
            for h in range(2):
                tx = (x + dx) % NX
                src, dst = finx.at[e, x, tx * 2 + h], kvg.at[x, rows]
                if dx > 0:
                    act(copy(src, dst, KVR + e, dev(tx, z, h, lo, hi)))
                else:
                    mine = own & (hi == h)

                    @pl.when(jnp.logical_not(mine))
                    def _():
                        act(copy(src, dst, KVR + e, dev(tx, z, h, lo, hi)))

                    @pl.when(mine)
                    def _():
                        act(pltpu.make_async_copy(src, dst, rsem.at[KVR + e]))

    def r_end(e):
        if e == 0:
            for i in range(1, NZ):
                d_copy(i).wait_recv()
        for u in range(2):
            part = slice(u * 4, u * 4 + 4)
            t = terms(e, z, u)
            if e == 0:
                for i in range(1, NZ):
                    t = t + d_rx[i - 1, part].astype(F32)
            else:
                for d in range(2):
                    r_copy(d, 3, u).wait_recv()
                    t = t + rs_rx[d, 3, u].astype(F32)
            finx[e, x, part] = t.astype(BF)
        for i in range(2):
            sends.append(x_copy(e, i))
            sends[-1].start()
        to_owners(e, start)

    def x_forward(e):
        for i in range(2):
            x_copy(e, i).wait_recv()
            sends.append(x_copy(e, 2 + i))
            sends[-1].start()

    def turn_hidden():
        arrived(hid_buf, HID)
        for e in range(2):
            for i in range(4):
                cols = slice(i * 128, (i + 1) * 128)
                part = hid_buf[:, e * HALF : (e + 1) * HALF, cols].reshape(8 * HALF, 128)
                hid_t[e, cols, :] = part.astype(F32).T.astype(BF)

    z_end(0)
    sort_kv(0)
    to_groups(2, start)
    diagonal(0)
    z_step(1, 2)
    at = below(0, 2, (0, 1))
    z_step(1, 3)
    below(0, 5, at)

    d_send()
    z_end(1)
    sort_kv(1)
    diagonal(1)
    below(1, 7, (0, 1))
    r_step(0)
    r_end(0)

    def place_q(blk, c):
        for j in range(4):
            t = (dqt[blk, :, j * 128 : (j + 1) * 128] * 0.125).T
            for o in range(2):
                dqs[blk * 8 + j * 2 + o] = jnp.concatenate(
                    [t[o * 64 + h * 16 : o * 64 + h * 16 + 16] for h in range(4)], axis=1
                )
        return c

    lax.fori_loop(0, 8, place_q, 0)
    r_step(1)

    def give_q(i, c):
        for j in range(4):
            k = i * 4 + j
            dqs_tx[k] = dqs[stored[0, k * 2 + core]]
        return c

    lax.fori_loop(0, 8, give_q, 0)
    sends.append(copy(dqs_tx, dqs_rx, DQS, sib))
    sends[-1].start()
    x_forward(0)
    r_step(2)
    turn_hidden()
    r_step(3)

    def c_copy(i):
        g = (x + i) % NX
        return copy(wpart.at[1 - core, g], c_rx.at[g], CX + i, sib)

    def grad_w(e, i):
        g = (x + i) % NX
        r = dot(hid_t[e], finx[e, g].reshape(8 * HALF, 128)).reshape(32, 2, 8, 128)
        for c in range(2):
            part = r[:, c].reshape(256, 128)
            wpart[c, g] = part if e == 0 else wpart[c, g] + part
        if e == 1:
            sends.append(c_copy(i))
            sends[-1].start()

    for i in range(2):
        x_copy(0, 2 + i).wait_recv()
    for i in range(4):
        grad_w(0, i)
    r_end(1)

    arrived(dqs_rx, DQS)

    def add_q(i, c):
        for j in range(4):
            k = i * 4 + j
            dq_tx[k] = (dqs[stored[0, k * 2 + 1 - core]] + dqs_rx[k]).astype(BF)
        return c

    lax.fori_loop(0, 8, add_q, 0)
    rows, cols = pl.ds(pl.multiple_of(z * 16, 16), 16), pl.ds(pl.multiple_of(x * 256, 256), 256)

    def q_return(i):
        tx, tz = (x + i // NZ) % NX, (z + i) % NZ
        return copy(dq_tx.at[tx * 8 + tz], dq_out.at[rows, cols], DQ, dev(tx, tz, 1 - core, lo, hi))

    def return_q(i, c):
        q_return(i).start()
        return c

    lax.fori_loop(0, 32, return_q, 0)

    grad_w(1, 0)
    x_forward(1)
    grad_w(1, 3)
    grad_w(1, 1)
    for i in range(2):
        x_copy(1, 2 + i).wait_recv()
    grad_w(1, 2)
    for i in range(4):
        c_copy(i).wait_recv()

    def w_sum(g):
        return (wpart[core, g] + c_rx[g]).reshape(32, 8, 128)

    for i in range(2):
        w_tx[:, :, i * 128 : (i + 1) * 128] = jnp.concatenate([w_sum(i), w_sum(2 + i)], axis=1).astype(BF)

    def w_copy(i):
        tx, tz = (x + i // NZ) % NX, (z + i) % NZ
        return copy(w_tx.at[tx * 8 + tz], w_rx.at[z * 4 + hi * 2 + lo], WR, w_to(i))

    def send_w(i, c):
        w_copy(i).start()
        return c

    @pl.when(jnp.logical_not(stays))
    def _():
        w_copy(0).start()

    @pl.when(stays)
    def _():
        pltpu.make_async_copy(w_tx.at[x * 8 + z], w_rx.at[z * 4 + hi * 2 + lo], rsem.at[WR]).start()

    lax.fori_loop(1, 32, send_w, 0)

    for e in range(2):
        arrived(kvg.at[pl.ds(0, 2)], KVR + e)

    kv_grad = jnp.concatenate([kvg[g, :, :64] for g in range(4)] + [kvg[g, :, 64:] for g in range(4)], axis=1)
    for i in range(4):
        in_out[:, i * 512 : (i + 1) * 512] = lax.dot_general(
            kv_grad, w_all[i], NT, preferred_element_type=F32
        ).astype(BF)

    for i, buf in enumerate(bufs):
        copy(buf.at[got], buf.at[got], Q + i, sib).wait_send()
    copy(dq_tx, dq_tx, DQ, sib).wait_send()
    arrived(dq_tx, DQ)
    for c in sends:
        c.wait_send()

    def sent(c):
        if c.is_remote:
            c.wait_send()

    for i in range(3):
        to_groups(i, sent)
    for e in range(2):
        to_owners(e, sent)

    arrived(w_rx, WR)

    def add_w(i, t):
        return t + w_rx[i].astype(F32)

    total = lax.fori_loop(0, 32, add_w, jnp.zeros((16, 256), F32))
    groups = [total[r : r + 8, c : c + 128] for r in (0, 8) for c in (0, 128)]
    wg_out[...] = jnp.concatenate([g[:, :64] for g in groups] + [g[:, 64:] for g in groups], axis=1)

    @pl.when(stays)
    def _():
        part = w_tx.at[pl.ds(0, 31)]
        copy(part, part, WR, sib).wait_send()

    @pl.when(jnp.logical_not(stays))
    def _():
        copy(w_tx, w_tx, WR, sib).wait_send()


def backward(hid, w, q, do, stat, order):
    v = pltpu.VMEM
    return pl.pallas_call(
        backward_kernel,
        name="backward",
        out_shape=(
            jax.ShapeDtypeStruct((128, 1024), BF),
            jax.ShapeDtypeStruct((128, 2048), BF),
            jax.ShapeDtypeStruct((8, 512), F32),
        ),
        in_specs=[VMEM] * 6,
        out_specs=[VMEM] * 3,
        scratch_shapes=[
            v((1, 64), jnp.int32),
            v((1, 64), jnp.int32),
            v((64, 128), jnp.int32),
            pltpu.SMEM((1, 64), jnp.int32),
            pltpu.SMEM((64, 128), jnp.int32),
            v((4, 512, 512), BF),
            v((128, 512), F32),
            v((4, 128, 128), BF),
            v((64, 16, 256), BF),
            v((64, 16, 256), BF),
            v((64, 1, 128), F32),
            v((64, HALF, 128), BF),
            v((64, HALF, 128), BF),
            v((8, 64, 512), BF),
            v((8, 512, 128), BF),
            v((8, 512, 128), BF),
            v((8, 8 * HALF, 128), BF),
            v((8, 64, 8 * HALF), BF),
            v((8, 1, 512), F32),
            v((8, 1, 512), F32),
            v((8, 64, 512), F32),
            v((2, 64, HALF, 128), F32),
            v((4, 8 * HALF, 512), BF),
            v((4, 8 * HALF, 512), BF),
            v((64, 16, 256), F32),
            v((32, 16, 256), F32),
            v((32, 16, 256), F32),
            v((32, 16, 256), BF),
            v((7, 8, HALF, 128), BF),
            v((7, 8, HALF, 128), BF),
            v((2, 4, 2, 4, HALF, 128), BF),
            v((2, 4, 2, 4, HALF, 128), BF),
            v((2, 4, 8, HALF, 128), BF),
            v((4, 128, 128), BF),
            v((2, 512, 8 * HALF), BF),
            v((2, 4, 256, 128), F32),
            v((4, 256, 128), F32),
            v((32, 16, 256), BF),
            v((32, 16, 256), BF),
            pltpu.SemaphoreType.DMA((N_SEMS + 1,)),
            pltpu.SemaphoreType.DMA((N_SEMS,)),
        ],
        compiler_params=pltpu.CompilerParams(
            collective_id=0, has_side_effects=True, vmem_limit_bytes=56 * 2**20
        ),
    )(hid, w, q, do, stat, order)


def shards(hidden, queries, attn_out, grad_out, log_sums, block_order, w_kv):
    delta = jnp.sum(
        (grad_out[0].astype(F32) * attn_out[0].astype(F32)).reshape(128, Q_HEADS, HEAD_DIM), axis=2
    ).T

    stat = jnp.stack([log_sums[0], delta]).reshape(2, 4, 4, 8, 16).transpose(1, 3, 0, 2, 4).reshape(4, 8, 1, 128)
    dq_out, in_out, wg = backward(hidden[0], w_kv, queries[0], grad_out[0], stat, block_order)
    return dq_out[None], in_out[None], wg


def solution(mesh):
    return jax.shard_map(
        shards,
        mesh=mesh,
        in_specs=(
            P("fsdp", "ctx", None),
            P("fsdp", "ctx", None),
            P("fsdp", "ctx", None),
            P("fsdp", "ctx", None),
            P("fsdp", None, "ctx"),
            P("fsdp", None),
            P("fsdp", None),
        ),
        out_specs=(P("fsdp", "ctx", None), P("fsdp", "ctx", None), P(("fsdp", "ctx"), None)),
        check_vma=False,
    )
```

time: 131 us -> 118 us (0.901)
  Pallas kernels: 123 us -> 111 us
  other arithmetic: 2.26 us -> 0.11 us
    pallas_call x1, Pallas kernels: 123 us -> 111 us  [backward(): pl.pallas_call(backward_kernel, name='backward', out_shape=(jax.ShapeDtyp...]
    unnamed x15 -> x11, local copies, waits for them, and re-layouts: 4.25 us -> 4.47 us
where the time goes in v3:
time: 118 us
  Pallas kernels  111 us (94%)
  local copies, waits for them, and re-layouts  6.1 us (5%)
    pallas_call x1, Pallas kernels, backward(): pl.pallas_call(backward_kernel, name='backward', out_shape=(jax.ShapeDtyp...  111 us
    unnamed x11, local copies, waits for them, and re-layouts  4.47 us

profile of v3, /device:TPU:1, one launch (start us, length us, event | category | flops | bytes accessed | tf_op | source)
XLA Modules:
  0.0 117.8 jit_solution(167917726263602020)
XLA Ops:
  0.6 0.8 stack.8
  1.4 0.0 copy-start
  1.4 1.2 copy.12
  2.6 0.0 copy-done
  2.6 0.2 copy.11
  2.8 0.1 convert_multiply_fusion
  2.9 0.1 stack.9
  3.0 0.7 reshape.19.stat
  3.8 110.8 %backward.1 = (bf16[128,1024]{1,0:T(8,128)(2,1)}, bf16[128,2048]{1,0:T(8,128)(2,1)}, f32[8,512]{1,0:T(8,128)}) custom-call(bf16[128,2048]{1,0:T(8,128)(2,1)} %bitcast.11, bf16[512,512]{1,0:T(8,128)(2,1)} %w.1, bf16[128,1024]{1,0:T(8,128)(2,1)} %bitcast.14, bf16[128,1024]{1,0:T(8,128)(2,1)} %bitcast.10, f32[4,8,1,128]{3,2,1,0:T(1,128)} %reshape.19.stat, ...), custom_call_target="tpu_custom_call" | custom-call | tf_op jit(solution)/shard_map/backward/pallas_call | solution.py:604
  114.6 0.0 copy-start.1
  114.6 1.7 %copy.17 = bf16[1,128,1024]{2,1,0:T(8,128)(2,1)} copy(bf16[1,128,1024]{2,1,0:T(8,128)(2,1)} %bitcast.13) | data formatting | bytes 524288
  116.3 0.0 copy-done.1
  116.3 0.0 copy-start.2
  116.4 0.8 copy.18
  117.1 0.0 copy-done.2
  117.1 0.6 copy.19
  (3 shorter events, 0.1 us)
Async XLA Ops:
  1.4 1.2 %copy-start = (bf16[1,128,1024]{2,1,0:T(8,128)(2,1)S(1)}, bf16[1,128,1024]{2,1,0:T(8,128)(2,1)}, u32[]{:S(2)}) copy-start(bf16[1,128,1024]{2,1,0:T(8,128)(2,1)} %param.10) | copy-start | bytes 786436
  114.6 1.7 %copy-start.1 = (bf16[128,2048]{1,0:T(8,128)(2,1)S(1)}, bf16[128,2048]{1,0:T(8,128)(2,1)}, u32[]{:S(2)}) copy-start(bf16[128,2048]{1,0:T(8,128)(2,1)} %get-tuple-element.7) | copy-start | bytes 1572868
  116.3 0.8 copy-start.2

commit v4 on v3

--- a/solution.py
+++ b/solution.py
@@ -35,16 +35,16 @@
     pl.semaphore_signal(pltpu.get_barrier_semaphore(), inc=1, device_id=to, device_id_type=MESH)
 
 META, W, WF, Q, QF, KV, HID, ZG, ZR, DQS, DQ, KVR, XA, CX, WR = (
-    0, 1, 4, 6, 9, 12, 16, 17, 49, 81, 82, 83, 85, 93, 97
+    0, 98, 103, 6, 9, 12, 16, 17, 49, 81, 82, 83, 85, 93, 97
 )
-N_SEMS = 98
+N_SEMS = 107
 HALF = 32
 
 
 def backward_kernel(
-    hid, w, q, do, stat, mine_order,
+    hid, w, q, do, ao, ls, mine_order,
     dq_out, in_out, wg_out,
-    sib_order, stored_vm, sorted_vm, stored, sorted_, w_all, acc, kvs, q_buf, do_buf, stat_buf, kv_buf0, kv_buf1, hid_buf,
+    stat, sib_order, stored_vm, sorted_vm, stored, sorted_, w_all, acc, kvs, q_buf, do_buf, stat_buf, kv_buf0, kv_buf1, hid_buf,
     qz, dz, ks, kts, lse, dlt, dqt, dkv, pbufs, dbufs,
     dqs, dqs_tx, dqs_rx, dq_tx, d_tx, d_rx, rs_tx, rs_rx, finx, kvg, hid_t, wpart, c_rx, w_tx, w_rx,
     ssem, rsem,
@@ -110,13 +110,16 @@
 
     w_own = pltpu.make_async_copy(w, w_all.at[f], ssem.at[N_SEMS])
     w_own.start()
-    half = w.shape[0] // 2
+    quarter = w.shape[0] // 4
+
+    def w_rows(i):
+        return pl.ds(i * quarter, quarter)
+
     sends = [
-        copy(w.at[pl.ds(0, half)], w_all.at[f, pl.ds(0, half)], W, near),
-        copy(w.at[pl.ds(half, half)], w_all.at[f, pl.ds(half, half)], W + 1, far),
-        copy(w, w_all.at[f], W + 2, sib),
-        copy(mine_order, sib_order, META, sib),
+        copy(w.at[w_rows(i)], w_all.at[f, w_rows(i)], W + i, far if i % 2 else near) for i in range(4)
     ]
+    sends.append(copy(w, w_all.at[f], W + 4, sib))
+    sends.append(copy(mine_order, sib_order, META, sib))
     for c in sends:
         c.start()
 
@@ -129,7 +132,6 @@
         return (
             copy(q.at[rows, cols], q_buf.at[slot], Q, to),
             copy(do.at[rows, cols], do_buf.at[slot], Q + 1, to),
-            copy(stat.at[tx, tz], stat_buf.at[slot], Q + 2, to),
         )
 
     def send_q(i, c):
@@ -139,23 +141,53 @@
 
     lax.fori_loop(0, 32, send_q, 0)
 
+    prod = do[...].astype(F32) * ao[...].astype(F32)
+    heads = lax.broadcasted_iota(jnp.int32, (Q_HEADS, Q_HEADS * HEAD_DIM), 0)
+    pick = (lax.broadcasted_iota(jnp.int32, heads.shape, 1) // HEAD_DIM == heads).astype(F32).astype(BF)
+    delta = jnp.zeros((Q_HEADS, 128), F32)
+    for _ in range(3):
+        term = prod.astype(BF)
+        delta = delta + lax.dot_general(pick, term, NT, preferred_element_type=F32)
+        prod = prod - term.astype(F32)
+    turned = [[t] + [pltpu.roll(t, 16 * s, 1) for s in range(1, 8)] for t in (ls[...], delta)]
+    head_of = lax.broadcasted_iota(jnp.int32, (Q_HEADS, 128), 0) % 4
+    lanes_of = lax.broadcasted_iota(jnp.int32, (Q_HEADS, 128), 1) // 16
+    for tz in range(NZ):
+        row = jnp.zeros((Q_HEADS, 128), F32)
+        for k in range(2):
+            for h in range(4):
+                row = jnp.where(
+                    (head_of == h) & (lanes_of == h + 4 * k), turned[k][(h + 4 * k - tz) % 8], row
+                )
+        row = row + pltpu.roll(row, Q_HEADS - 1, 0)
+        row = row + pltpu.roll(row, Q_HEADS - 2, 0)
+        for g in range(4):
+            stat[g, tz] = row[4 * g : 4 * g + 1, :]
+
+    def send_stat(i, c):
+        tx, tz = (x + i // NZ) % NX, (z + i) % NZ
+        copy(stat.at[tx, tz], stat_buf.at[slot], Q + 2, dev(tx, tz, core, lo, 1 - hi)).start()
+        return c
+
+    lax.fori_loop(0, 32, send_stat, 0)
+
     def project(chunk):
         cols = pl.ds(pl.multiple_of(chunk * 512, 512), 512)
         return jnp.dot(hid[:, cols], w_all[chunk], preferred_element_type=F32)
 
     w_own.wait()
     acc[...] = project(f)
-    arrived(w_all.at[0], W + 2)
+    arrived(w_all.at[0], W + 4)
     acc[...] += project(lo * 2 + 1 - core)
     other, last = (1 - lo) * 2 + core, (1 - lo) * 2 + 1 - core
-    for i in range(2):
-        part = w_all.at[other, pl.ds(i * half, half)]
+    for i in range(4):
+        part = w_all.at[other, w_rows(i)]
         arrived(part, W + i)
         sends.append(copy(part, part, WF + i, sib))
         sends[-1].start()
     acc[...] += project(other)
-    for i in range(2):
-        arrived(w_all.at[last, pl.ds(i * half, half)], WF + i)
+    for i in range(4):
+        arrived(w_all.at[last, w_rows(i)], WF + i)
     key_vals = (acc[...] + project(last)).astype(BF)
     for g in range(KV_HEADS):
         kvs[g] = jnp.concatenate(
@@ -226,7 +258,6 @@
     z_step(1, 0)
     z_step(0, 2)
     z_step(0, 3)
-    z_step(1, 1)
 
     got = pl.ds(pl.multiple_of((1 - core) * 32, 32), 32)
     theirs = pl.ds(pl.multiple_of(core * 32, 32), 32)
@@ -276,6 +307,7 @@
         return c
 
     lax.fori_loop(0, 8, sort_q, 0)
+    z_step(1, 1)
 
     def sort_kv(e):
         def one(blk, c):
@@ -332,8 +364,10 @@
         wrap = c == 7
         return jnp.where(wrap, m + 1, m), jnp.where(wrap, jnp.minimum(m + 2, 7), c + 1)
 
-    def below(e, n, at):
+    def below(e, n, at, beside=None):
         def four(i, at):
+            if beside is not None:
+                beside(i)
             tiles = [at]
             for t in range(4):
                 probs(*tiles[t], t)
@@ -429,13 +463,19 @@
             sends.append(x_copy(e, 2 + i))
             sends[-1].start()
 
-    def turn_hidden():
-        arrived(hid_buf, HID)
-        for e in range(2):
-            for i in range(4):
-                cols = slice(i * 128, (i + 1) * 128)
-                part = hid_buf[:, e * HALF : (e + 1) * HALF, cols].reshape(8 * HALF, 128)
-                hid_t[e, cols, :] = part.astype(F32).T.astype(BF)
+    def turn_hidden(i):
+        e, c = i // 4, i % 4
+        cols = pl.ds(pl.multiple_of(c * 128, 128), 128)
+        part = hid_buf[:, pl.ds(pl.multiple_of(e * HALF, HALF), HALF), cols].reshape(8 * HALF, 128)
+        hid_t[e, cols, :] = part.astype(F32).T.astype(BF)
+
+    def place_q(blk):
+        for j in range(4):
+            t = (dqt[blk, :, j * 128 : (j + 1) * 128] * 0.125).T
+            for o in range(2):
+                dqs[blk * 8 + j * 2 + o] = jnp.concatenate(
+                    [t[o * 64 + h * 16 : o * 64 + h * 16 + 16] for h in range(4)], axis=1
+                )
 
     z_end(0)
     sort_kv(0)
@@ -450,20 +490,19 @@
     z_end(1)
     sort_kv(1)
     diagonal(1)
-    below(1, 7, (0, 1))
+    arrived(hid_buf, HID)
+    turn_hidden(7)
+
+    def beside(i):
+        turn_hidden(i)
+        place_q(jnp.maximum(i - 1, 0))
+
+    below(1, 7, (0, 1), beside)
     r_step(0)
     r_end(0)
 
-    def place_q(blk, c):
-        for j in range(4):
-            t = (dqt[blk, :, j * 128 : (j + 1) * 128] * 0.125).T
-            for o in range(2):
-                dqs[blk * 8 + j * 2 + o] = jnp.concatenate(
-                    [t[o * 64 + h * 16 : o * 64 + h * 16 + 16] for h in range(4)], axis=1
-                )
-        return c
-
-    lax.fori_loop(0, 8, place_q, 0)
+    for blk in (6, 7):
+        place_q(blk)
     r_step(1)
 
     def give_q(i, c):
@@ -477,7 +516,27 @@
     sends[-1].start()
     x_forward(0)
     r_step(2)
-    turn_hidden()
+    arrived(dqs_rx, DQS)
+
+    def add_q(i, c):
+        for j in range(4):
+            k = i * 4 + j
+            dq_tx[k] = (dqs[stored[0, k * 2 + 1 - core]] + dqs_rx[k]).astype(BF)
+        return c
+
+    lax.fori_loop(0, 8, add_q, 0)
+    rows, cols = pl.ds(pl.multiple_of(z * 16, 16), 16), pl.ds(pl.multiple_of(x * 256, 256), 256)
+
+    def q_return(i):
+        tx, tz = (x + i // NZ) % NX, (z + i) % NZ
+        return copy(dq_tx.at[tx * 8 + tz], dq_out.at[rows, cols], DQ, dev(tx, tz, 1 - core, lo, hi))
+
+    def return_q(i, c):
+        q_return(i).start()
+        return c
+
+    lax.fori_loop(0, 32, return_q, 0)
+
     r_step(3)
 
     def c_copy(i):
@@ -500,27 +559,6 @@
         grad_w(0, i)
     r_end(1)
 
-    arrived(dqs_rx, DQS)
-
-    def add_q(i, c):
-        for j in range(4):
-            k = i * 4 + j
-            dq_tx[k] = (dqs[stored[0, k * 2 + 1 - core]] + dqs_rx[k]).astype(BF)
-        return c
-
-    lax.fori_loop(0, 8, add_q, 0)
-    rows, cols = pl.ds(pl.multiple_of(z * 16, 16), 16), pl.ds(pl.multiple_of(x * 256, 256), 256)
-
-    def q_return(i):
-        tx, tz = (x + i // NZ) % NX, (z + i) % NZ
-        return copy(dq_tx.at[tx * 8 + tz], dq_out.at[rows, cols], DQ, dev(tx, tz, 1 - core, lo, hi))
-
-    def return_q(i, c):
-        q_return(i).start()
-        return c
-
-    lax.fori_loop(0, 32, return_q, 0)
-
     grad_w(1, 0)
     x_forward(1)
     grad_w(1, 3)
@@ -599,7 +637,7 @@
         copy(w_tx, w_tx, WR, sib).wait_send()
 
 
-def backward(hid, w, q, do, stat, order):
+def backward(hid, w, q, do, ao, ls, order):
     v = pltpu.VMEM
     return pl.pallas_call(
         backward_kernel,
@@ -609,9 +647,10 @@
             jax.ShapeDtypeStruct((128, 2048), BF),
             jax.ShapeDtypeStruct((8, 512), F32),
         ),
-        in_specs=[VMEM] * 6,
+        in_specs=[VMEM] * 7,
         out_specs=[VMEM] * 3,
         scratch_shapes=[
+            v((4, 8, 1, 128), F32),
             v((1, 64), jnp.int32),
             v((1, 64), jnp.int32),
             v((64, 128), jnp.int32),
@@ -657,16 +696,11 @@
         compiler_params=pltpu.CompilerParams(
             collective_id=0, has_side_effects=True, vmem_limit_bytes=56 * 2**20
         ),
-    )(hid, w, q, do, stat, order)
+    )(hid, w, q, do, ao, ls, order)
 
 
 def shards(hidden, queries, attn_out, grad_out, log_sums, block_order, w_kv):
-    delta = jnp.sum(
-        (grad_out[0].astype(F32) * attn_out[0].astype(F32)).reshape(128, Q_HEADS, HEAD_DIM), axis=2
-    ).T
-
-    stat = jnp.stack([log_sums[0], delta]).reshape(2, 4, 4, 8, 16).transpose(1, 3, 0, 2, 4).reshape(4, 8, 1, 128)
-    dq_out, in_out, wg = backward(hidden[0], w_kv, queries[0], grad_out[0], stat, block_order)
+    dq_out, in_out, wg = backward(hidden[0], w_kv, queries[0], grad_out[0], attn_out[0], log_sums[0], block_order)
     return dq_out[None], in_out[None], wg
 
 

time: 118 us -> 115 us (0.975)
  local copies, waits for them, and re-layouts: 6.1 us -> 3.13 us
    unnamed x11 -> x7, local copies, waits for them, and re-layouts: 4.47 us -> 3.13 us
where the time goes in v4:
time: 115 us
  Pallas kernels  111 us (97%)
  local copies, waits for them, and re-layouts  3.13 us (3%)
    pallas_call x1, Pallas kernels, backward(): pl.pallas_call(backward_kernel, name='backward', out_shape=(jax.ShapeDtyp...  111 us
    unnamed x7, local copies, waits for them, and re-layouts  3.13 us

profile of v4, /device:TPU:1, one launch (start us, length us, event | category | flops | bytes accessed | tf_op | source)
XLA Modules:
  0.0 114.9 jit_solution(12530581888902669964)
XLA Ops:
  0.6 111.1 %backward.1 = (bf16[128,1024]{1,0:T(8,128)(2,1)}, bf16[128,2048]{1,0:T(8,128)(2,1)}, f32[8,512]{1,0:T(8,128)}) custom-call(bf16[128,2048]{1,0:T(8,128)(2,1)} %bitcast.8, bf16[512,512]{1,0:T(8,128)(2,1)} %w.1, bf16[128,1024]{1,0:T(8,128)(2,1)} %bitcast.10, bf16[128,1024]{1,0:T(8,128)(2,1)} %bitcast.11, bf16[128,1024]{1,0:T(8,128)(2,1)} %bitcast.12, ...), custom_call_target="tpu_custom_call" | custom-call | tf_op jit(solution)/shard_map/backward/pallas_call | solution.py:642
  111.8 0.0 copy-start
  111.8 1.7 %copy.13 = bf16[1,128,1024]{2,1,0:T(8,128)(2,1)} copy(bf16[1,128,1024]{2,1,0:T(8,128)(2,1)} %bitcast.9) | data formatting | bytes 524288
  113.5 0.0 copy-done
  113.5 0.0 copy-start.1
  113.5 0.8 copy.14
  114.3 0.0 copy-done.1
  114.3 0.6 copy.15
Async XLA Ops:
  111.8 1.7 %copy-start = (bf16[128,2048]{1,0:T(8,128)(2,1)S(1)}, bf16[128,2048]{1,0:T(8,128)(2,1)}, u32[]{:S(2)}) copy-start(bf16[128,2048]{1,0:T(8,128)(2,1)} %get-tuple-element.7) | copy-start | bytes 1572868
  113.5 0.8 copy-start.1

commit v5 on v4

--- a/solution.py
+++ b/solution.py
@@ -13,6 +13,7 @@
 MESH = pl.DeviceIdType.MESH
 Q_HEADS, KV_HEADS, HEAD_DIM = 16, 4, 64
 NX, NZ = 4, 8
+Z_STEPS = (4, 1, 7, 3, 5, 2, 6, 0)
 VMEM = pl.BlockSpec(memory_space=pltpu.VMEM)
 
 
@@ -72,10 +73,11 @@
         greet(to)
 
     def greet_q(i, c):
-        greet(dev((x + i // NZ) % NX, (z + i) % NZ, 1 - core, lo, hi))
-        return c
-
-    lax.fori_loop(0, 32, greet_q, 0)
+        for j in range(4):
+            greet(dev((x + i // 2) % NX, (z + i * 4 + j) % NZ, 1 - core, lo, hi))
+        return c
+
+    lax.fori_loop(0, 8, greet_q, 0)
 
     def greet_kv(i, c):
         dx, h = i // 2, i % 2
@@ -97,13 +99,17 @@
         return dev((x + i // NZ) % NX, (z + i) % NZ, core, x // 2, x % 2)
 
     def greet_w(i, c):
-        @pl.when(jnp.logical_not(stays & (i == 0)))
-        def _():
-            greet(w_from(i))
-
-        return c
-
-    lax.fori_loop(0, 32, greet_w, 0)
+        for j in range(4):
+            greet(w_from(i * 4 + j))
+        return c
+
+    @pl.when(jnp.logical_not(stays))
+    def _():
+        greet(w_from(0))
+
+    for i in range(1, 4):
+        greet(w_from(i))
+    lax.fori_loop(1, 8, greet_w, 0)
     pl.semaphore_wait(
         pltpu.get_barrier_semaphore(), 12 + 32 + 8 + 32 - own.astype(jnp.int32) - stays.astype(jnp.int32)
     )
@@ -135,11 +141,71 @@
         )
 
     def send_q(i, c):
-        for one in q_copies(i):
-            one.start()
-        return c
-
-    lax.fori_loop(0, 32, send_q, 0)
+        for j in Z_STEPS:
+            for one in q_copies(i * NZ + j):
+                one.start()
+        return c
+
+    lax.fori_loop(0, NX, send_q, 0)
+
+    def project(chunk):
+        cols = pl.ds(pl.multiple_of(chunk * 512, 512), 512)
+        return jnp.dot(hid[:, cols], w_all[chunk], preferred_element_type=F32)
+
+    w_own.wait()
+    acc[...] = project(f)
+    arrived(w_all.at[0], W + 4)
+    acc[...] += project(lo * 2 + 1 - core)
+    other, last = (1 - lo) * 2 + core, (1 - lo) * 2 + 1 - core
+    for i in range(4):
+        part = w_all.at[other, w_rows(i)]
+        arrived(part, W + i)
+        sends.append(copy(part, part, WF + i, sib))
+        sends[-1].start()
+    acc[...] += project(other)
+    for i in range(4):
+        arrived(w_all.at[last, w_rows(i)], WF + i)
+    key_vals = (acc[...] + project(last)).astype(BF)
+    for g in range(KV_HEADS):
+        kvs[g] = jnp.concatenate(
+            [key_vals[:, g * 64 : g * 64 + 64], key_vals[:, 256 + g * 64 : 320 + g * 64]], axis=1
+        )
+
+    kv_buf = (kv_buf0, kv_buf1)
+
+    def to_group(dx, j, which):
+        tx = (x + dx) % NX
+        to = dev(tx, z, core, lo, j)
+        mine = x * 2 + hi
+        if which < 2:
+            rows = pl.ds(j * 64 + which * HALF, HALF)
+            return (kvs.at[tx, rows], kv_buf[which].at[z * 8 + mine], KV + which * 2 + x // 2), to
+        rows, cols = pl.ds(j * 64, 64), pl.ds(pl.multiple_of(tx * 512, 512), 512)
+        return (hid.at[rows, cols], hid_buf.at[mine], HID), to
+
+    def to_groups(which, act):
+        for dx in range(NX):
+            for j in range(2):
+                piece, to = to_group(dx, j, which)
+                if dx > 0:
+                    act(copy(*piece, to))
+                else:
+                    mine = own & (core == j)
+
+                    @pl.when(jnp.logical_not(mine))
+                    def _():
+                        act(copy(*piece, to))
+
+                    @pl.when(mine)
+                    def _():
+                        src, dst, sem = piece
+                        act(pltpu.make_async_copy(src, dst, rsem.at[sem]))
+
+    def start(c):
+        c.start()
+
+    to_groups(0, start)
+    to_groups(1, start)
 
     prod = do[...].astype(F32) * ao[...].astype(F32)
     heads = lax.broadcasted_iota(jnp.int32, (Q_HEADS, Q_HEADS * HEAD_DIM), 0)
@@ -165,70 +231,13 @@
             stat[g, tz] = row[4 * g : 4 * g + 1, :]
 
     def send_stat(i, c):
-        tx, tz = (x + i // NZ) % NX, (z + i) % NZ
-        copy(stat.at[tx, tz], stat_buf.at[slot], Q + 2, dev(tx, tz, core, lo, 1 - hi)).start()
-        return c
-
-    lax.fori_loop(0, 32, send_stat, 0)
-
-    def project(chunk):
-        cols = pl.ds(pl.multiple_of(chunk * 512, 512), 512)
-        return jnp.dot(hid[:, cols], w_all[chunk], preferred_element_type=F32)
-
-    w_own.wait()
-    acc[...] = project(f)
-    arrived(w_all.at[0], W + 4)
-    acc[...] += project(lo * 2 + 1 - core)
-    other, last = (1 - lo) * 2 + core, (1 - lo) * 2 + 1 - core
-    for i in range(4):
-        part = w_all.at[other, w_rows(i)]
-        arrived(part, W + i)
-        sends.append(copy(part, part, WF + i, sib))
-        sends[-1].start()
-    acc[...] += project(other)
-    for i in range(4):
-        arrived(w_all.at[last, w_rows(i)], WF + i)
-    key_vals = (acc[...] + project(last)).astype(BF)
-    for g in range(KV_HEADS):
-        kvs[g] = jnp.concatenate(
-            [key_vals[:, g * 64 : g * 64 + 64], key_vals[:, 256 + g * 64 : 320 + g * 64]], axis=1
-        )
-
-    kv_buf = (kv_buf0, kv_buf1)
-
-    def to_group(dx, j, which):
-        tx = (x + dx) % NX
-        to = dev(tx, z, core, lo, j)
-        mine = x * 2 + hi
-        if which < 2:
-            rows = pl.ds(j * 64 + which * HALF, HALF)
-            return (kvs.at[tx, rows], kv_buf[which].at[z * 8 + mine], KV + which * 2 + x // 2), to
-        rows, cols = pl.ds(j * 64, 64), pl.ds(pl.multiple_of(tx * 512, 512), 512)
-        return (hid.at[rows, cols], hid_buf.at[mine], HID), to
-
-    def to_groups(which, act):
-        for dx in range(NX):
-            for j in range(2):
-                piece, to = to_group(dx, j, which)
-                if dx > 0:
-                    act(copy(*piece, to))
-                else:
-                    mine = own & (core == j)
-
-                    @pl.when(jnp.logical_not(mine))
-                    def _():
-                        act(copy(*piece, to))
-
-                    @pl.when(mine)
-                    def _():
-                        src, dst, sem = piece
-                        act(pltpu.make_async_copy(src, dst, rsem.at[sem]))
-
-    def start(c):
-        c.start()
-
-    to_groups(0, start)
-    to_groups(1, start)
+        for j in Z_STEPS:
+            tx, tz = (x + i) % NX, (z + j) % NZ
+            copy(stat.at[tx, tz], stat_buf.at[slot], Q + 2, dev(tx, tz, core, lo, 1 - hi)).start()
+        return c
+
+    lax.fori_loop(0, NX, send_stat, 0)
+
 
     def z_part(src_z, u):
         return pl.ds(pl.multiple_of(src_z * 8 + u * 4, 4), 4)
@@ -407,7 +416,7 @@
         return copy(d_tx.at[i - 1], d_rx.at[i - 1], ZR + i, zdev(i))
 
     def d_send():
-        for i in (4, 3, 5, 2, 6, 1, 7):
+        for i in Z_STEPS[:-1]:
             for u in range(2):
                 d_tx[i - 1, u * 4 : u * 4 + 4] = terms(0, (z + i) % NZ, u).astype(BF)
             sends.append(d_copy(i))
@@ -532,10 +541,11 @@
         return copy(dq_tx.at[tx * 8 + tz], dq_out.at[rows, cols], DQ, dev(tx, tz, 1 - core, lo, hi))
 
     def return_q(i, c):
-        q_return(i).start()
-        return c
-
-    lax.fori_loop(0, 32, return_q, 0)
+        for j in Z_STEPS:
+            q_return(i * NZ + j).start()
+        return c
+
+    lax.fori_loop(0, NX, return_q, 0)
 
     r_step(3)
 
@@ -580,7 +590,8 @@
         return copy(w_tx.at[tx * 8 + tz], w_rx.at[z * 4 + hi * 2 + lo], WR, w_to(i))
 
     def send_w(i, c):
-        w_copy(i).start()
+        for j in Z_STEPS:
+            w_copy(i * NZ + j).start()
         return c
 
     @pl.when(jnp.logical_not(stays))
@@ -591,7 +602,9 @@
     def _():
         pltpu.make_async_copy(w_tx.at[x * 8 + z], w_rx.at[z * 4 + hi * 2 + lo], rsem.at[WR]).start()
 
-    lax.fori_loop(1, 32, send_w, 0)
+    for i in Z_STEPS[:-1]:
+        w_copy(i).start()
+    lax.fori_loop(1, NX, send_w, 0)
 
     for e in range(2):
         arrived(kvg.at[pl.ds(0, 2)], KVR + e)

time: 115 us -> 115 us (level)
  no operation moved by 1% of the time
where the time goes in v5:
time: 115 us
  Pallas kernels  111 us (97%)
  local copies, waits for them, and re-layouts  3.13 us (3%)
    pallas_call x1, Pallas kernels, backward(): pl.pallas_call(backward_kernel, name='backward', out_shape=(jax.ShapeDtyp...  111 us
    unnamed x7, local copies, waits for them, and re-layouts  3.13 us

profile of v5, /device:TPU:1, one launch (start us, length us, event | category | flops | bytes accessed | tf_op | source)
XLA Modules:
  0.0 114.9 jit_solution(17134424103127695494)
XLA Ops:
  0.6 111.1 %backward.1 = (bf16[128,1024]{1,0:T(8,128)(2,1)}, bf16[128,2048]{1,0:T(8,128)(2,1)}, f32[8,512]{1,0:T(8,128)}) custom-call(bf16[128,2048]{1,0:T(8,128)(2,1)} %bitcast.8, bf16[512,512]{1,0:T(8,128)(2,1)} %w.1, bf16[128,1024]{1,0:T(8,128)(2,1)} %bitcast.10, bf16[128,1024]{1,0:T(8,128)(2,1)} %bitcast.11, bf16[128,1024]{1,0:T(8,128)(2,1)} %bitcast.12, ...), custom_call_target="tpu_custom_call" | custom-call | tf_op jit(solution)/shard_map/backward/pallas_call | solution.py:655
  111.7 0.0 copy-start
  111.7 1.7 %copy.13 = bf16[1,128,1024]{2,1,0:T(8,128)(2,1)} copy(bf16[1,128,1024]{2,1,0:T(8,128)(2,1)} %bitcast.9) | data formatting | bytes 524288
  113.4 0.0 copy-done
  113.5 0.0 copy-start.1
  113.5 0.8 copy.14
  114.2 0.0 copy-done.1
  114.3 0.6 copy.15
Async XLA Ops:
  111.7 1.7 %copy-start = (bf16[128,2048]{1,0:T(8,128)(2,1)S(1)}, bf16[128,2048]{1,0:T(8,128)(2,1)}, u32[]{:S(2)}) copy-start(bf16[128,2048]{1,0:T(8,128)(2,1)} %get-tuple-element.7) | copy-start | bytes 1572868
  113.5 0.8 copy-start.1

commit v6 on v5

--- a/solution.py
+++ b/solution.py
@@ -508,11 +508,9 @@
 
     below(1, 7, (0, 1), beside)
     r_step(0)
-    r_end(0)
 
     for blk in (6, 7):
         place_q(blk)
-    r_step(1)
 
     def give_q(i, c):
         for j in range(4):
@@ -523,8 +521,10 @@
     lax.fori_loop(0, 8, give_q, 0)
     sends.append(copy(dqs_tx, dqs_rx, DQS, sib))
     sends[-1].start()
+    r_step(1)
+    r_end(0)
+    r_step(2)
     x_forward(0)
-    r_step(2)
     arrived(dqs_rx, DQS)
 
     def add_q(i, c):

time: 115 us -> 115 us (level)
  no operation moved by 1% of the time
where the time goes in v6:
time: 115 us
  Pallas kernels  111 us (97%)
  local copies, waits for them, and re-layouts  3.13 us (3%)
    pallas_call x1, Pallas kernels, backward(): pl.pallas_call(backward_kernel, name='backward', out_shape=(jax.ShapeDtyp...  111 us
    unnamed x7, local copies, waits for them, and re-layouts  3.13 us

profile of v6, /device:TPU:1, one launch (start us, length us, event | category | flops | bytes accessed | tf_op | source)
XLA Modules:
  0.0 114.8 jit_solution(4696418131912134105)
XLA Ops:
  0.6 111.0 %backward.1 = (bf16[128,1024]{1,0:T(8,128)(2,1)}, bf16[128,2048]{1,0:T(8,128)(2,1)}, f32[8,512]{1,0:T(8,128)}) custom-call(bf16[128,2048]{1,0:T(8,128)(2,1)} %bitcast.8, bf16[512,512]{1,0:T(8,128)(2,1)} %w.1, bf16[128,1024]{1,0:T(8,128)(2,1)} %bitcast.10, bf16[128,1024]{1,0:T(8,128)(2,1)} %bitcast.11, bf16[128,1024]{1,0:T(8,128)(2,1)} %bitcast.12, ...), custom_call_target="tpu_custom_call" | custom-call | tf_op jit(solution)/shard_map/backward/pallas_call | solution.py:655
  111.7 0.0 copy-start
  111.7 1.7 %copy.13 = bf16[1,128,1024]{2,1,0:T(8,128)(2,1)} copy(bf16[1,128,1024]{2,1,0:T(8,128)(2,1)} %bitcast.9) | data formatting | bytes 524288
  113.4 0.0 copy-done
  113.4 0.0 copy-start.1
  113.4 0.8 copy.14
  114.2 0.0 copy-done.1
  114.2 0.6 copy.15
Async XLA Ops:
  111.7 1.7 %copy-start = (bf16[128,2048]{1,0:T(8,128)(2,1)S(1)}, bf16[128,2048]{1,0:T(8,128)(2,1)}, u32[]{:S(2)}) copy-start(bf16[128,2048]{1,0:T(8,128)(2,1)} %get-tuple-element.7) | copy-start | bytes 1572868
  113.4 0.8 copy-start.1
